TPU v7x, 512 devices: a whole 4x4x16 slice. The times are simulated.
512 devices in a mesh: dom: 32 (over y, x, core), own: 16 (over z).
Axes of the slice: x: 4, y: 4, z: 16, core: 2. Of those that a mesh axis runs over, the one named last changes fastest.
Arguments:
- tiles: bfloat16 [57344, 128, 128], P(('dom', 'own')), may hold values from -0.75 to 0.75
- prolong: bfloat16 [192, 128, 128], P('dom'), may hold values from -0.5 to 0.5
- features: bfloat16 [192, 128, 128], P('dom'), may hold values from -0.1875 to 0.1875
- match: int32 [192], P('dom'), may hold values from 0 to 2, as said below
- row_local: int32 [57344], P(('dom', 'own')), may hold values from 0 to 5
- col_dom: int32 [57344, 1], P(('dom', 'own')), may hold values from 0 to 31; in each aligned block of 112 rows (0 to 111, 112 to 223, ...) at most 4 rows name the same one
- col_local: int32 [57344], P(('dom', 'own')), may hold values from 0 to 5
- coarse_slot: int32 [57344], P(('dom', 'own')), may hold values from 0 to 31
- tile_count: int32 [512], P(('dom', 'own')), may hold values from 14 to 112, as said below
Outputs:
- coarse_tiles: float32 [1024, 128, 128], P(('dom', 'own'))
- coarse_features: float32 [12288, 128], P(('dom', 'own'))
Inputs may be any that keep to these rules, and one draw needn't show every extreme that they name: `match`: within the 6 entries of each dom index every value appears exactly twice: the heavy-edge matching pairs fine blocks into coarse blocks. `col_dom`: among the 112 slots of one device at most 4 name the same dom index. `tile_count`: some device has all 112 slots live.
All inputs are finite; a program needn't handle non-finite values.
Results may differ from a plain program's by a relative error of at most 0.0029.
Values may be sent and summed in bfloat16 or wider, within the bound.
No kernel may reach another device: no remote copies, remote signals or barrier semaphores. Data moves between devices by JAX's collectives and lax.ppermute only.
A program may use at most 64 MiB of HBM per device.

v0:
```python
import jax
import jax.numpy as jnp
from jax import lax
from jax.sharding import PartitionSpec as P

CS_OWN = 2


def local(tiles, prolong, features, match, row_local, col_dom, col_local, coarse_slot, tile_count):
    owners = lax.axis_size("own")
    count = tiles.shape[0]
    blocks_here = prolong.shape[0]
    width = tiles.shape[1]
    feat_width = features.shape[2]
    slots_all = CS_OWN * owners
    target = col_dom[:, 0]
    source_p, source_x = (
        lax.all_gather(prolong, "dom", axis=0, tiled=True),
        lax.all_gather(features, "dom", axis=0, tiled=True),
    )
    where = target * blocks_here + col_local
    valid = (jnp.arange(count, dtype=jnp.int32) < tile_count[0]).astype(jnp.float32)
    coarse = match[row_local]
    turns = count // 16
    items = (
        tiles.reshape(turns, 16, width, width),
        row_local.reshape(turns, 16),
        where.reshape(turns, 16),
        coarse_slot.reshape(turns, 16),
        coarse.reshape(turns, 16),
        valid.reshape(turns, 16),
    )

    def accumulate(carry, piece):
        tile_sums, feat_sums = carry
        block_tiles, rows, spot, slot, group, keep = piece
        left = jnp.einsum(
            "tki,tkj->tij", prolong[rows], block_tiles, preferred_element_type=jnp.float32
        ).astype(jnp.bfloat16)
        right = (
            jnp.einsum("tik,tkj->tij", left, source_p[spot], preferred_element_type=jnp.float32)
            * keep[:, None, None]
        )
        feat = (
            jnp.einsum("tik,tkf->tif", left, source_x[spot], preferred_element_type=jnp.float32)
            * keep[:, None, None]
        )
        tile_sums = tile_sums.at[slot].add(right)
        feat_sums = feat_sums.at[group].add(feat)
        return ((tile_sums, feat_sums), None)

    start = (
        jnp.zeros((slots_all, width, width), jnp.float32),
        jnp.zeros((blocks_here // 2, width, feat_width), jnp.float32),
    )
    (tile_sums, feat_sums), _ = lax.scan(accumulate, start, items)
    feat_flat = feat_sums.reshape(blocks_here // 2 * width, feat_width)
    coarse_tiles, coarse_features = (
        lax.psum_scatter(tile_sums, "own", scatter_dimension=0, tiled=True),
        lax.psum_scatter(feat_flat, "own", scatter_dimension=0, tiled=True),
    )
    return (coarse_tiles, coarse_features)


def solution(mesh):
    placed = (
        P(("dom", "own"), None, None),
        P("dom", None, None),
        P("dom", None, None),
        P("dom"),
        P(("dom", "own")),
        P(("dom", "own"), None),
        P(("dom", "own")),
        P(("dom", "own")),
        P(("dom", "own")),
    )
    return jax.shard_map(
        local,
        mesh=mesh,
        in_specs=placed,
        out_specs=(P(("dom", "own"), None, None), P(("dom", "own"), None)),
        check_vma=False,
    )
```

profile of v0, /device:TPU:6, one launch (start us, length us, event | category | flops | bytes accessed | tf_op | source)
XLA Modules:
  0.0 406.7 jit_solution(10473511967326218119)
XLA Ops:
  11.6 4.2 %compare_select_fusion.5 = s32[112]{0:T(128)S(1)} fusion(s32[112]{0:T(128)} %param.15, s32[]{:T(128)} %bitcast.13, s32[]{:T(128)} %bitcast.14, s32[]{:T(128)} %bitcast.15, s32[]{:T(128)} %bitcast.16, s32[]{:T(128)} %bitcast.17, s32[]{:T(128)} %bitcast.18), kind=kLoop, calls=%fused_computation.34 | loop fusion | flops 1456 | bytes 920 | tf_op jit(solution)/shard_map/gather | solution.py:23
  17.4 61.8 %all-gather.5.cloned.1.call-done = bf16[192,128,128]{2,1,0:T(8,128)(2,1)} async-done(((bf16[6,128,128]{2,1,0:T(8,128)(2,1)}), bf16[192,128,128]{2,1,0:T(8,128)(2,1)}) %all-gather.5.cloned.1.call-update) | async-done | bytes 6291472 | tf_op jit(solution)/shard_map/all_gather | solution.py:19
  79.2 66.7 %all-gather.3.cloned.1.call-done = bf16[192,128,128]{2,1,0:T(8,128)(2,1)} async-done(((bf16[6,128,128]{2,1,0:T(8,128)(2,1)}), bf16[192,128,128]{2,1,0:T(8,128)(2,1)}) %all-gather.3.cloned.1.call-update) | async-done | bytes 6291472 | tf_op jit(solution)/shard_map/all_gather | solution.py:18
  147.5 108.5 %while.12 = (s32[]{:T(128)}, f32[32,128,128]{2,1,0:T(8,128)}, f32[3,128,128]{2,1,0:T(8,128)S(1)}, s32[7,16]{1,0:T(8,128)S(1)}, s32[7,16]{1,0:T(8,128)S(1)}, /*in...) while((s32[]{:T(128)}, f32[32,128,128]{2,1,0:T(8,128)}, ...), condition=%wide.region_3.4_spmd, body=%wide.region_0.3_spmd.sunk | while | flops 202639552 | bytes 15213909 | solution.py:56
  150.5 3.4 gather_fusion.2
  154.0 3.4 gather_fusion.1
  159.6 3.4 scatter_fusion
  166.1 3.4 gather_fusion.2
  169.5 3.4 gather_fusion.1
  175.1 3.4 scatter_fusion
  181.6 3.4 gather_fusion.2
  185.0 3.4 gather_fusion.1
  190.7 3.4 scatter_fusion
  197.1 3.4 gather_fusion.2
  200.5 3.4 gather_fusion.1
  212.6 3.4 gather_fusion.2
  216.0 3.4 gather_fusion.1
  221.7 3.4 scatter_fusion
  228.1 3.4 gather_fusion.2
  231.5 3.4 gather_fusion.1
  243.6 3.4 gather_fusion.2
  247.0 3.4 gather_fusion.1
  257.2 68.3 %reduce-scatter.7.cloned.1.call-done = f32[24,128]{1,0:T(8,128)} async-done(((f32[384,128]{1,0:T(8,128)}), f32[24,128]{1,0:T(8,128)}) %reduce-scatter.7.cloned.1.call-update) | async-done | bytes 12304
  325.5 74.6 %reduce-scatter.5.cloned.1.call-done = f32[2,128,128]{2,1,0:T(8,128)} async-done(((f32[32,128,128]{2,1,0:T(8,128)}), f32[2,128,128]{2,1,0:T(8,128)}) %reduce-scatter.5.cloned.1.call-update) | async-done | bytes 131088 | tf_op jit(solution)/shard_map/reduce_scatter | solution.py:59
  (92 shorter events, 54.5 us)
Async XLA Ops:
  7.2 72.0 %all-gather.5.cloned.1.call-start = ((), (), s32[]{:S(2)}) async-start(), calls=%async_computation.3 | async-start | bytes 6488064 | tf_op jit(solution)/shard_map/all_gather | solution.py:19
  7.9 138.0 %all-gather.3.cloned.1.call-start = ((), (), s32[]{:S(2)}) async-start(), calls=%async_computation.2 | async-start | bytes 6488064 | tf_op jit(solution)/shard_map/all_gather | solution.py:18
  8.6 316.9 %reduce-scatter.7.cloned.1.call-start = ((), (), s32[]{:S(2)}) async-start(), calls=%async_computation.5 | async-start | bytes 208896
  256.0 0.7 copy-start
  256.7 143.5 %reduce-scatter.5.cloned.1.call-start = ((), (), s32[]{:S(2)}) async-start(), calls=%async_computation.4 | async-start | bytes 2228224 | tf_op jit(solution)/shard_map/reduce_scatter | solution.py:59
Sparse Core Ops, SparseCore 0:
  11.1 68.0 all-gather.4
  82.3 63.5 all-gather.2
  256.8 68.6 reduce-scatter.6
  329.0 71.1 reduce-scatter.4
where the time goes:
time: 408 us; the launch traced here: 407 us
  waiting for transfers between devices  273 us (67%)
  local copies, waits for them, and re-layouts  64.5 us (16%)
  other arithmetic  39.9 us (10%)
  between operations  14.4 us (4%)
  matrix products  13.9 us (3%)
    reduce_scatter x1, waiting for transfers between devices, local(): lax.psum_scatter(tile_sums, 'own', scatter_dimension=0, tiled=True)  74.6 us
    unnamed x5, waiting for transfers between devices  70.2 us
    all_gather x1, waiting for transfers between devices, local(): lax.all_gather(prolong, 'dom', axis=0, tiled=True)  66.7 us
    all_gather x1, waiting for transfers between devices, local(): lax.all_gather(features, 'dom', axis=0, tiled=True)  61.8 us
    gather x7, local copies, waits for them, and re-layouts, accumulate(): source_x[spot]  24 us
    gather x7, local copies, waits for them, and re-layouts, accumulate(): source_p[spot]  24 us
    scatter-add x7, other arithmetic, accumulate(): tile_sums = tile_sums.at[slot].add(right)  23.5 us
    scatter-add x7, other arithmetic, accumulate(): feat_sums = feat_sums.at[group].add(feat)  11.2 us
  transfers between devices with their start and end apart: 4, of which 4 were waited for; matrix products, arithmetic and copies ran while one was open for 2% of the time, Pallas kernels for 0%

commit v1 on v0

v1 whole, which is shorter than its diff:
```python
import jax
import jax.numpy as jnp
from jax import lax
from jax.experimental import pallas as pl
from jax.experimental.pallas import tpu as pltpu
from jax.sharding import PartitionSpec as P

OWN = 16
STEP = 16
UNROLL = 4
BF = jnp.bfloat16
F32 = jnp.float32


def left_kernel(rows, count, prolong, tiles, left, turned):
    step = pl.program_id(0)

    @pl.when(step == 0)
    def _():
        for r in range(prolong.shape[0]):
            turned[r] = prolong[r].T

    @pl.when(step * STEP < count[0])
    def _():
        for k in range(STEP):
            row = rows[step * STEP + k]
            left[k] = jnp.dot(turned[row], tiles[k], preferred_element_type=F32).astype(BF)


def left_products(rows, count, prolong, tiles):
    total, width, _ = tiles.shape

    def block(i, rows, count):
        return (jnp.minimum(i, (count[0] - 1) // STEP), 0, 0)

    return pl.pallas_call(
        left_kernel,
        grid_spec=pltpu.PrefetchScalarGridSpec(
            num_scalar_prefetch=2,
            grid=(total // STEP,),
            in_specs=[
                pl.BlockSpec(prolong.shape, lambda i, rows, count: (0, 0, 0)),
                pl.BlockSpec((STEP, width, width), block),
            ],
            out_specs=pl.BlockSpec((STEP, width, width), block),
            scratch_shapes=[pltpu.VMEM(prolong.shape, BF)],
        ),
        out_shape=jax.ShapeDtypeStruct(tiles.shape, BF),
        compiler_params=pltpu.CompilerParams(vmem_limit_bytes=32 << 20),
        cost_estimate=pl.CostEstimate(flops=2 * total * width**3, bytes_accessed=4 * total * width**2, transcendentals=0),
        name="left_products",
    )(rows, count, prolong, tiles)


def column_kernel(where, slot, group, count, left, blocks, out, held_l, held_b, sums, feats, sem_l, sem_b):
    live = count[0]
    turns = pl.cdiv(live, UNROLL)

    def copies(t):
        return (
            pltpu.make_async_copy(left.at[t], held_l.at[t], sem_l.at[t]),
            pltpu.make_async_copy(blocks.at[where[t]], held_b.at[t], sem_b.at[t]),
        )

    @pl.loop(0, turns * UNROLL)
    def _(t):
        for c in copies(t):
            c.start()

    sums[...] = jnp.zeros_like(sums)
    feats[...] = jnp.zeros_like(feats)
    spare_slot = sums.shape[0] - 1
    spare_group = feats.shape[0] // 128 - 1

    @pl.loop(0, turns)
    def _(i):
        for u in range(UNROLL):
            for c in copies(i * UNROLL + u):
                c.wait()
        for u in range(UNROLL):
            t = i * UNROLL + u
            both = jnp.dot(held_l[t], held_b[t], preferred_element_type=F32)
            s = jnp.where(t < live, slot[t], spare_slot)
            g = jnp.where(t < live, group[t], spare_group)
            rows = pl.ds(pl.multiple_of(g * 128, 128), 128)
            sums[s] += both[:, :128]
            feats[rows, :] += both[:, 128:]

    for o in range(OWN):
        out[280 * o : 280 * o + 128, :] = sums[2 * o]
        out[280 * o + 128 : 280 * o + 256, :] = sums[2 * o + 1]
        out[280 * o + 256 : 280 * o + 280, :] = feats[24 * o : 24 * o + 24, :]


def column_products(where, slot, group, count, left, blocks):
    total = left.shape[0]
    smem = pl.BlockSpec(memory_space=pltpu.SMEM)
    return pl.pallas_call(
        column_kernel,
        in_specs=[smem] * 4 + [pl.BlockSpec(memory_space=pl.ANY)] * 2,
        out_specs=pl.BlockSpec(memory_space=pltpu.VMEM),
        out_shape=jax.ShapeDtypeStruct((OWN * 280, 128), F32),
        scratch_shapes=[
            pltpu.VMEM((total, 128, 128), BF),
            pltpu.VMEM((total, 128, 256), BF),
            pltpu.VMEM((33, 128, 128), F32),
            pltpu.VMEM((4 * 128, 128), F32),
            pltpu.SemaphoreType.DMA((total,)),
            pltpu.SemaphoreType.DMA((total,)),
        ],
        compiler_params=pltpu.CompilerParams(vmem_limit_bytes=48 << 20),
        cost_estimate=pl.CostEstimate(flops=4 * total * 128**3, bytes_accessed=12 << 20, transcendentals=0),
        name="column_products",
    )(where, slot, group, count, left, blocks)


def local(tiles, prolong, features, match, row_local, col_dom, col_local, coarse_slot, tile_count):
    here = prolong.shape[0]
    blocks = lax.all_gather(jnp.concatenate([prolong, features], axis=2), "dom", axis=0, tiled=True)
    left = left_products(row_local, tile_count, prolong, tiles)
    where = col_dom[:, 0] * here + col_local
    group = match[row_local]
    sums = column_products(where, coarse_slot, group, tile_count, left, blocks)
    mine = lax.psum_scatter(sums, "own", scatter_dimension=0, tiled=True)
    return mine[:256].reshape(2, 128, 128), mine[256:]


def solution(mesh):
    placed = (
        P(("dom", "own"), None, None),
        P("dom", None, None),
        P("dom", None, None),
        P("dom"),
        P(("dom", "own")),
        P(("dom", "own"), None),
        P(("dom", "own")),
        P(("dom", "own")),
        P(("dom", "own")),
    )
    return jax.shard_map(
        local,
        mesh=mesh,
        in_specs=placed,
        out_specs=(P(("dom", "own"), None, None), P(("dom", "own"), None)),
        check_vma=False,
    )
```

time: 408 us -> 268 us (0.66)
  local copies, waits for them, and re-layouts: 64.5 us -> 12.3 us
  waiting for transfers between devices: 273 us -> 223 us
  other arithmetic: 39.9 us -> 5.55 us
  matrix products: 13.9 us -> 0 us
  Pallas kernels: 0 us -> 12 us
    unnamed x5 -> x3, waiting for transfers between devices: 70.2 us -> 150 us
    reduce_scatter x1 -> x0, waiting for transfers between devices: 74.6 us -> none  [local(): lax.psum_scatter(tile_sums, 'own', scatter_dimension=0, tiled=True)]
    gather x22 -> x1, local copies, waits for them, and re-layouts: 60.6 us -> 0.67 us  [local(): group = match[row_local]]
    all_gather x2 -> x1, waiting for transfers between devices: 128 us -> 72.1 us  [local(): lax.all_gather(jnp.concatenate([prolong, features], axis=2), 'dom', axis=...]
    scatter-add x14 -> x0, other arithmetic: 34.7 us -> none  [the longest x7 23.5 us: accumulate(): tile_sums = tile_sums.at[slot].add(right)]
    dot_general x21 -> x0, matrix products: 13.9 us -> none  [the longest x7 9.78 us: accumulate(): jnp.einsum('tki,tkj->tij', prolong[rows], block_tiles, preferred_element_...]
    pallas_call x0 -> x2, Pallas kernels: none -> 12 us  [the longest x1 9.99 us: column_products(): pl.pallas_call(column_kernel, in_specs=[smem] * 4 + [pl.BlockSpec(memory_...]
    unnamed x2 -> x19, local copies, waits for them, and re-layouts: 0.67 us -> 8.72 us
  transfers between devices with their start and end apart: 4 -> 2, of which waited for: 4 -> 2; matrix products, arithmetic and copies ran while one was open for 2% -> 2% of each run, Pallas kernels for 0% -> 1%
where the time goes in v1:
time: 268 us
  waiting for transfers between devices  223 us (83%)
  between operations  15.4 us (6%)
  local copies, waits for them, and re-layouts  12.3 us (5%)
  Pallas kernels  12 us (4%)
  other arithmetic  5.55 us (2%)
    unnamed x3, waiting for transfers between devices  150 us
    all_gather x1, waiting for transfers between devices, local(): lax.all_gather(jnp.concatenate([prolong, features], axis=2), 'dom', axis=...  72.1 us
    pallas_call x1, Pallas kernels, column_products(): pl.pallas_call(column_kernel, in_specs=[smem] * 4 + [pl.BlockSpec(memory_...  9.99 us
    unnamed x19, local copies, waits for them, and re-layouts  8.72 us
  transfers between devices with their start and end apart: 2, of which 2 were waited for; matrix products, arithmetic and copies ran while one was open for 2% of the time, Pallas kernels for 1%

profile of v1, /device:TPU:6, one launch (start us, length us, event | category | flops | bytes accessed | tf_op | source)
XLA Modules:
  0.0 267.9 jit_solution(9301301858030660472)
XLA Ops:
  7.2 0.0 all-gather.2.cloned.1.call-start
  7.2 1.8 pad_maximum_fusion
  9.0 0.0 all-gather.2.cloned.1.call-update
  9.1 0.0 all-reduce.3.cloned.1.call-start
  9.8 0.0 copy-start.2
  9.8 2.0 copy-done.2
  11.8 0.9 copy-done.3
  12.7 0.7 copy-done.4
  13.4 2.0 left_products.1.left
  15.5 0.0 copy-start
  15.5 1.8 copy-done
  17.3 0.0 copy-done.6
  17.3 0.7 fusion
  17.9 0.0 copy-done.7
  17.9 3.7 %compare_select_fusion.1 = (s32[112]{0:T(128)S(1)}, s32[112]{0:T(128)S(1)}) fusion(s32[112]{0:T(128)S(1)} %copy-done.4, s32[]{:T(128)} %bitcast.1, s32[]{:T(128)} %bitcast.2, s32[]{:T(128)} %bitcast.3, s32[]{:T(128)} %bitcast.4, s32[]{:T(128)} %bitcast.5, s32[]{:T(128)} %bitcast.6, s32[112]{0:T(128)S(1)} %copy-done.7, s32[112,1]{0,1:T(1,128)S(1)} %copy-done.8), kind=kLoop, calls=%fused_computation.2 | loop fusion | flops 1680 | bytes 2264 | tf_op jit(solution)/shard_map/gather | solution.py:122
  21.7 72.1 %all-gather.2.cloned.1.call-done.blocks = bf16[192,128,256]{2,1,0:T(8,128)(2,1)} async-done(((bf16[6,128,256]{2,1,0:T(8,128)(2,1)}), bf16[192,128,256]{2,1,0:T(8,128)(2,1)}) %all-gather.2.cloned.1.call-update) | async-done | bytes 12582928 | tf_op jit(solution)/shard_map/all_gather | solution.py:119
  93.8 0.0 copy-done.5
  93.8 2.0 copy-done.1
  95.8 10.0 %column_products.1 = f32[4480,128]{1,0:T(8,128)} custom-call(s32[112]{0:T(128)S(1)} %get-tuple-element.9.where, s32[112]{0:T(128)S(1)} %copy-done.5, s32[112]{0:T(128)S(1)} %get-tuple-element.8.group, s32[1]{0:T(128)S(6)} %copy.12.count, bf16[112,128,128]{2,1,0:T(8,128)(2,1)S(1)} %copy-done.1, bf16[192,128,256]{2,1,0:T(8,128)(2,1)} %all-gather.2.cloned.1.call-done.blocks), custom_call_target="tpu_custom_call" | custom-call | flops 939524096 | bytes 12582912 | tf_op jit(solution)/shard_map/column_products/pallas_call | solution.py:98
  105.8 0.0 all-reduce.3.cloned.1.call-update
  105.8 1.3 dynamic-slice
  107.8 150.4 %all-reduce.3.cloned.1.call-done = f32[4480,128]{1,0:T(8,128)} async-done(((f32[4480,128]{1,0:T(8,128)}), f32[4480,128]{1,0:T(8,128)}) %all-reduce.3.cloned.1.call-update) | async-done | bytes 2293776
  258.2 1.6 constant_dynamic-slice_fusion
  259.8 1.3 constant_dynamic-slice_fusion.1
  (8 shorter events, 0.0 us)
Async XLA Ops:
  7.2 86.6 %all-gather.2.cloned.1.call-start = ((), (), s32[]{:S(2)}) async-start(), calls=%async_computation | async-start | bytes 12976128 | tf_op jit(solution)/shard_map/all_gather | solution.py:119
  9.1 249.1 %all-reduce.3.cloned.1.call-start = ((), (), s32[]{:S(2)}) async-start(), calls=%async_computation.1 | async-start | bytes 4587520
  9.8 2.0 copy-start.2
  11.8 0.9 copy-start.3
  12.7 0.7 copy-start.4
  13.4 3.9 %copy-start.6 = (s32[6]{0:T(128)S(1)}, s32[6]{0:T(128)}, u32[]{:S(2)}) copy-start(s32[6]{0:T(128)} %param.12) | copy-start | bytes 76
  13.4 4.5 %copy-start.7 = (s32[112]{0:T(128)S(1)}, s32[112]{0:T(128)}, u32[]{:S(2)}) copy-start(s32[112]{0:T(128)} %param.15) | copy-start | bytes 1348
  13.4 4.5 %copy-start.8 = (s32[112,1]{0,1:T(1,128)S(1)}, s32[112,1]{0,1:T(1,128)}, u32[]{:S(2)}) copy-start(s32[112,1]{0,1:T(1,128)} %param.14) | copy-start | bytes 1348
  13.4 80.4 %copy-start.5 = (s32[112]{0:T(128)S(1)}, s32[112]{0:T(128)}, u32[]{:S(2)}) copy-start(s32[112]{0:T(128)} %slot.1) | copy-start | bytes 1348
  15.5 1.8 copy-start
  93.8 2.0 copy-start.1
Sparse Core Ops, SparseCore 0:
  11.1 82.6 all-gather.1
  106.0 152.2 all-reduce.2

commit v2 on v1

--- a/solution.py
+++ b/solution.py
@@ -6,6 +6,8 @@
 from jax.sharding import PartitionSpec as P
 
 OWN = 16
+HALF = OWN // 2
+PART = 144
 STEP = 16
 UNROLL = 4
 BF = jnp.bfloat16
@@ -52,7 +54,7 @@
     )(rows, count, prolong, tiles)
 
 
-def column_kernel(where, slot, group, count, left, blocks, out, held_l, held_b, sums, feats, sem_l, sem_b):
+def column_kernel(where, slot, group, count, parity, left, blocks, up, down, keep_a, keep_b, held_l, held_b, sums, feats, sem_l, sem_b):
     live = count[0]
     turns = pl.cdiv(live, UNROLL)
 
@@ -86,20 +88,29 @@
             sums[s] += both[:, :128]
             feats[rows, :] += both[:, 128:]
 
-    for o in range(OWN):
-        out[280 * o : 280 * o + 128, :] = sums[2 * o]
-        out[280 * o + 128 : 280 * o + 256, :] = sums[2 * o + 1]
-        out[280 * o + 256 : 280 * o + 280, :] = feats[24 * o : 24 * o + 24, :]
-
-
-def column_products(where, slot, group, count, left, blocks):
+    p = parity[0]
+
+    def put(ref, k, owner, part):
+        ref[k, 0:128] = sums[2 * owner + part].astype(ref.dtype)
+        rows = pl.ds(pl.multiple_of(24 * owner + 16 * part, 8), 16)
+        ref[k, 128:144] = feats[rows, :].astype(ref.dtype)
+
+    for k in range(HALF):
+        put(up, k, 2 * k + 1 - p, p)
+        put(down, k, 2 * k + 1 - p, 1 - p)
+        put(keep_a, k, 2 * k + p, p)
+        put(keep_b, k, 2 * k + p, 1 - p)
+
+
+def column_products(where, slot, group, count, parity, left, blocks):
     total = left.shape[0]
     smem = pl.BlockSpec(memory_space=pltpu.SMEM)
+    shape = (HALF, PART, 128)
     return pl.pallas_call(
         column_kernel,
-        in_specs=[smem] * 4 + [pl.BlockSpec(memory_space=pl.ANY)] * 2,
-        out_specs=pl.BlockSpec(memory_space=pltpu.VMEM),
-        out_shape=jax.ShapeDtypeStruct((OWN * 280, 128), F32),
+        in_specs=[smem] * 5 + [pl.BlockSpec(memory_space=pl.ANY)] * 2,
+        out_specs=[pl.BlockSpec(memory_space=pltpu.VMEM)] * 4,
+        out_shape=[jax.ShapeDtypeStruct(shape, t) for t in (BF, BF, F32, F32)],
         scratch_shapes=[
             pltpu.VMEM((total, 128, 128), BF),
             pltpu.VMEM((total, 128, 256), BF),
@@ -111,7 +122,53 @@
         compiler_params=pltpu.CompilerParams(vmem_limit_bytes=48 << 20),
         cost_estimate=pl.CostEstimate(flops=4 * total * 128**3, bytes_accessed=12 << 20, transcendentals=0),
         name="column_products",
-    )(where, slot, group, count, left, blocks)
+    )(where, slot, group, count, parity, left, blocks)
+
+
+def pair_kernel(keep_a, above, keep_b, below, out):
+    out[:, :PART] = (keep_a[...] + above[...].astype(F32)).astype(BF)
+    out[:, PART:] = (keep_b[...] + below[...].astype(F32)).astype(BF)
+
+
+def pair_sums(keep_a, above, keep_b, below):
+    return pl.pallas_call(
+        pair_kernel,
+        out_shape=jax.ShapeDtypeStruct((HALF, 2 * PART, 128), BF),
+        compiler_params=pltpu.CompilerParams(vmem_limit_bytes=16 << 20),
+        name="pair_sums",
+    )(keep_a, above, keep_b, below)
+
+
+def last_kernel(parity, parts, tiles, feats):
+    p = parity[0]
+    total = parts[0].astype(F32)
+    for k in range(1, HALF):
+        total += parts[k].astype(F32)
+    tiles[p] = total[0:128]
+    tiles[1 - p] = total[PART : PART + 128]
+    first, second = total[128:PART], total[PART + 128 :]
+    feats[0:16] = jnp.where(p == 0, first, second)
+    feats[16:24] = jnp.where(p == 0, second, first)[0:8]
+
+
+def last_sums(parity, parts):
+    return pl.pallas_call(
+        last_kernel,
+        in_specs=[pl.BlockSpec(memory_space=pltpu.SMEM), pl.BlockSpec(memory_space=pltpu.VMEM)],
+        out_specs=[pl.BlockSpec(memory_space=pltpu.VMEM)] * 2,
+        out_shape=[jax.ShapeDtypeStruct((2, 128, 128), F32), jax.ShapeDtypeStruct((24, 128), F32)],
+        compiler_params=pltpu.CompilerParams(vmem_limit_bytes=16 << 20),
+        name="last_sums",
+    )(parity, parts)
+
+
+def own_sums(parity, up, down, keep_a, keep_b):
+    below = lax.ppermute(up, "own", [(z, (z + 1) % OWN) for z in range(OWN)])
+    above = lax.ppermute(down, "own", [(z, (z - 1) % OWN) for z in range(OWN)])
+    mid = pair_sums(keep_a, above, keep_b, below)
+    groups = [[2 * k + b for k in range(HALF)] for b in range(2)]
+    parts = lax.all_to_all(mid, "own", 0, 0, tiled=True, axis_index_groups=groups)
+    return last_sums(parity, parts)
 
 
 def local(tiles, prolong, features, match, row_local, col_dom, col_local, coarse_slot, tile_count):
@@ -120,9 +177,9 @@
     left = left_products(row_local, tile_count, prolong, tiles)
     where = col_dom[:, 0] * here + col_local
     group = match[row_local]
-    sums = column_products(where, coarse_slot, group, tile_count, left, blocks)
-    mine = lax.psum_scatter(sums, "own", scatter_dimension=0, tiled=True)
-    return mine[:256].reshape(2, 128, 128), mine[256:]
+    parity = jnp.reshape(lax.axis_index("own") % 2, (1,)).astype(jnp.int32)
+    up, down, keep_a, keep_b = column_products(where, coarse_slot, group, tile_count, parity, left, blocks)
+    return own_sums(parity, up, down, keep_a, keep_b)
 
 
 def solution(mesh):

time: 268 us -> 179 us (0.67)
  waiting for transfers between devices: 223 us -> 79.5 us
  blocking collectives: 0 us -> 47.7 us
  starting transfers between devices: 0.08 us -> 14.3 us
  local copies, waits for them, and re-layouts: 12.3 us -> 8.11 us
  Pallas kernels: 12 us -> 8.69 us
    unnamed x3 -> x1, waiting for transfers between devices: 150 us -> 0.02 us
    all_to_all x0 -> x1, blocking collectives: none -> 47.7 us  [own_sums(): lax.all_to_all(mid, 'own', 0, 0, tiled=True, axis_index_groups=groups)]
    ppermute x0 -> x2, starting transfers between devices: none -> 14.2 us  [the longest x1 8.17 us: own_sums(): above = lax.ppermute(down, 'own', [(z, (z - 1) % OWN) for z in range(OWN)])]
    ppermute x0 -> x2, waiting for transfers between devices: none -> 6.86 us  [the longest x1 5.66 us: own_sums(): above = lax.ppermute(down, 'own', [(z, (z - 1) % OWN) for z in range(OWN)])]
    slice x2 -> x0, local copies, waits for them, and re-layouts: 2.89 us -> none  [local(): return (mine[:256].reshape(2, 128, 128), mine[256:])]
    pallas_call x1 -> x3, Pallas kernels: 9.99 us -> 7.22 us  [the longest x1 6.39 us: column_products(): pl.pallas_call(column_kernel, in_specs=[smem] * 5 + [pl.BlockSpec(memory_...]
    unnamed x19 -> x18, local copies, waits for them, and re-layouts: 8.72 us -> 7.44 us
  transfers between devices with their start and end apart: 2 -> 3, of which waited for: 2 -> 3; matrix products, arithmetic and copies ran while one was open for 2% -> 2% of each run, Pallas kernels for 1% -> 1%
where the time goes in v2:
time: 179 us
  waiting for transfers between devices  79.5 us (44%)
  blocking collectives  47.7 us (27%)
  between operations  14.8 us (8%)
  starting transfers between devices  14.3 us (8%)
  Pallas kernels  8.69 us (5%)
  local copies, waits for them, and re-layouts  8.11 us (5%)
  other arithmetic  5.63 us (3%)
    all_gather x1, waiting for transfers between devices, local(): lax.all_gather(jnp.concatenate([prolong, features], axis=2), 'dom', axis=...  72.7 us
    all_to_all x1, blocking collectives, own_sums(): lax.all_to_all(mid, 'own', 0, 0, tiled=True, axis_index_groups=groups)  47.7 us
    ppermute x1, starting transfers between devices, own_sums(): above = lax.ppermute(down, 'own', [(z, (z - 1) % OWN) for z in range(OWN)])  8.17 us
    unnamed x18, local copies, waits for them, and re-layouts  7.44 us
    pallas_call x1, Pallas kernels, column_products(): pl.pallas_call(column_kernel, in_specs=[smem] * 5 + [pl.BlockSpec(memory_...  6.39 us
    ppermute x1, starting transfers between devices, own_sums(): below = lax.ppermute(up, 'own', [(z, (z + 1) % OWN) for z in range(OWN)])  6.06 us
    ppermute x1, waiting for transfers between devices, own_sums(): above = lax.ppermute(down, 'own', [(z, (z - 1) % OWN) for z in range(OWN)])  5.66 us
    gather x1, other arithmetic, local(): group = match[row_local]  3.8 us
  transfers between devices with their start and end apart: 3, of which 3 were waited for; matrix products, arithmetic and copies ran while one was open for 2% of the time, Pallas kernels for 1%

profile of v2, /device:TPU:6, one launch (start us, length us, event | category | flops | bytes accessed | tf_op | source)
XLA Modules:
  0.0 178.7 jit_solution(9974256706208976971)
XLA Ops:
  7.2 0.0 all-gather.2.cloned.1.call-start
  7.2 1.8 %pad_maximum_fusion = bf16[6,128,256]{2,1,0:T(8,128)(2,1)} fusion(bf16[6,128,128]{2,1,0:T(8,128)(2,1)} %param.11, bf16[6,128,128]{2,1,0:T(8,128)(2,1)} %prolong.1), kind=kLoop, calls=%fused_computation | loop fusion | flops 786432 | bytes 786432 | tf_op jit(solution)/shard_map/concatenate | solution.py:176
  9.0 0.0 all-gather.2.cloned.1.call-update
  9.7 0.0 copy-start.2
  9.7 2.0 %copy-done.2 = bf16[112,128,128]{2,1,0:T(8,128)(2,1)S(1)} copy-done((bf16[112,128,128]{2,1,0:T(8,128)(2,1)S(1)}, bf16[112,128,128]{2,1,0:T(8,128)(2,1)}, u32[]{:S(2)}) %copy-start.2) | copy-done | bytes 3670040
  11.8 0.9 copy-done.3
  12.7 0.7 copy-done.4
  13.4 1.5 left_products.1.left
  14.8 0.0 copy-start
  14.8 1.8 copy-done
  16.6 0.7 fusion
  17.3 0.0 copy-done.8
  17.3 3.8 %compare_select_fusion.1 = (s32[112]{0:T(128)S(1)}, s32[112]{0:T(128)S(1)}) fusion(s32[112]{0:T(128)S(1)} %copy-done.4, s32[]{:T(128)} %bitcast.2, s32[]{:T(128)} %bitcast.3, s32[]{:T(128)} %bitcast.4, s32[]{:T(128)} %bitcast.5, s32[]{:T(128)} %bitcast.6, s32[]{:T(128)} %bitcast.7, s32[112]{0:T(128)S(1)} %copy-done.7, s32[112,1]{0,1:T(1,128)S(1)} %copy-done.8), kind=kLoop, calls=%fused_computation.2 | loop fusion | flops 1680 | bytes 2264 | tf_op jit(solution)/shard_map/gather | solution.py:179
  21.1 72.7 %all-gather.2.cloned.1.call-done.blocks = bf16[192,128,256]{2,1,0:T(8,128)(2,1)} async-done(((bf16[6,128,256]{2,1,0:T(8,128)(2,1)}), bf16[192,128,256]{2,1,0:T(8,128)(2,1)}) %all-gather.2.cloned.1.call-update) | async-done | bytes 12582928 | tf_op jit(solution)/shard_map/all_gather | solution.py:176
  93.8 0.0 copy-done.5
  93.8 2.0 %copy-done.1 = bf16[112,128,128]{2,1,0:T(8,128)(2,1)S(1)} copy-done((bf16[112,128,128]{2,1,0:T(8,128)(2,1)S(1)}, bf16[112,128,128]{2,1,0:T(8,128)(2,1)}, u32[]{:S(2)}) %copy-start.1) | copy-done | bytes 3670040
  95.8 6.4 %column_products.1 = (bf16[8,144,128]{2,1,0:T(8,128)(2,1)S(1)}, bf16[8,144,128]{2,1,0:T(8,128)(2,1)S(1)}, f32[8,144,128]{2,1,0:T(8,128)S(1)}, f32[8,144,128]{2,1,0:T(8,128)S(1)}) custom-call(s32[112]{0:T(128)S(1)} %get-tuple-element.17.where, s32[112]{0:T(128)S(1)} %copy-done.5, s32[112]{0:T(128)S(1)} %get-tuple-element.16.group, s32[1]{0:T(128)S(6)} %copy.11.count, ...), custom_call_target="tpu_custom_call" | custom-call | flops 939524096 | bytes 12582912 | tf_op jit(solution)/shard_map/column_products/pallas_call | solution.py:109
  102.2 8.2 %collective-permute-start = (bf16[8,144,128]{2,1,0:T(8,128)(2,1)S(1)}, bf16[8,144,128]{2,1,0:T(8,128)(2,1)S(1)}, u32[]{:S(2)}, u32[]{:S(2)}) collective-permute-start(bf16[8,144,128]{2,1,0:T(8,128)(2,1)S(1)} %get-tuple-element.7), channel_id=1, source_target_pairs={{0,15},{1,0},{2,1},{3,2},{4,3},{5,4},{6,5},{7,6},{8,7},{9,8},{10,9... | collective-permute-start | bytes 884744 | tf_op jit(solution)/shard_map/ppermute | solution.py:167
  110.4 6.1 %collective-permute-start.1 = (bf16[8,144,128]{2,1,0:T(8,128)(2,1)S(1)}, bf16[8,144,128]{2,1,0:T(8,128)(2,1)S(1)}, u32[]{:S(2)}, u32[]{:S(2)}) collective-permute-start(bf16[8,144,128]{2,1,0:T(8,128)(2,1)S(1)} %get-tuple-element.9), channel_id=1, source_target_pairs={{0,1},{1,2},{2,3},{3,4},{4,5},{5,6},{6,7},{7,8},{8,9},{9,10},{10,1... | collective-permute-start | bytes 884744 | tf_op jit(solution)/shard_map/ppermute | solution.py:166
  116.5 5.7 %collective-permute-done.above = bf16[8,144,128]{2,1,0:T(8,128)(2,1)S(1)} collective-permute-done((bf16[8,144,128]{2,1,0:T(8,128)(2,1)S(1)}, bf16[8,144,128]{2,1,0:T(8,128)(2,1)S(1)}, u32[]{:S(2)}, u32[]{:S(2)}) %collective-permute-start) | collective-permute-done | bytes 294944 | tf_op jit(solution)/shard_map/ppermute | solution.py:167
  122.1 1.2 collective-permute-done.1.below
  123.3 0.1 pair_sums.1
  123.4 47.7 %all_to_all.5.parts = bf16[8,288,128]{2,1,0:T(8,128)(2,1)S(1)} all-to-all(bf16[8,288,128]{2,1,0:T(8,128)(2,1)S(1)} %pair_sums.1), channel_id=1, replica_groups={{0,2,4,6,8,10,12,14},{1,3,5,7,9,11,13,15},{16,18,20,22,24,26,28,30},{17..., dimensions={0} | all-to-all | bytes 1179648 | tf_op jit(solution)/shard_map/all_to_all | solution.py:170
  171.1 0.7 last_sums.1
  (9 shorter events, 0.0 us)
Async XLA Ops:
  7.2 86.6 %all-gather.2.cloned.1.call-start = ((), (), s32[]{:S(2)}) async-start(), calls=%async_computation.1 | async-start | bytes 12976128 | tf_op jit(solution)/shard_map/all_gather | solution.py:176
  9.7 2.0 %copy-start.2 = (bf16[112,128,128]{2,1,0:T(8,128)(2,1)S(1)}, bf16[112,128,128]{2,1,0:T(8,128)(2,1)}, u32[]{:S(2)}) copy-start(bf16[112,128,128]{2,1,0:T(8,128)(2,1)} %tiles.1) | copy-start | bytes 11010052
  11.8 0.9 copy-start.3
  12.7 0.7 copy-start.4
  13.3 3.3 %copy-start.6 = (s32[6]{0:T(128)S(1)}, s32[6]{0:T(128)}, u32[]{:S(2)}) copy-start(s32[6]{0:T(128)} %param.12) | copy-start | bytes 76
  13.3 3.9 %copy-start.7 = (s32[112]{0:T(128)S(1)}, s32[112]{0:T(128)}, u32[]{:S(2)}) copy-start(s32[112]{0:T(128)} %param.15) | copy-start | bytes 1348
  13.3 3.9 %copy-start.8 = (s32[112,1]{0,1:T(1,128)S(1)}, s32[112,1]{0,1:T(1,128)}, u32[]{:S(2)}) copy-start(s32[112,1]{0,1:T(1,128)} %param.14) | copy-start | bytes 1348
  13.4 80.4 %copy-start.5 = (s32[112]{0:T(128)S(1)}, s32[112]{0:T(128)}, u32[]{:S(2)}) copy-start(s32[112]{0:T(128)} %slot.1) | copy-start | bytes 1348
  14.8 1.8 copy-start
  93.8 2.0 %copy-start.1 = (bf16[112,128,128]{2,1,0:T(8,128)(2,1)S(1)}, bf16[112,128,128]{2,1,0:T(8,128)(2,1)}, u32[]{:S(2)}) copy-start(bf16[112,128,128]{2,1,0:T(8,128)(2,1)} %copy-done) | copy-start | bytes 11010052
  102.2 19.9 %collective-permute-start = (bf16[8,144,128]{2,1,0:T(8,128)(2,1)S(1)}, bf16[8,144,128]{2,1,0:T(8,128)(2,1)S(1)}, u32[]{:S(2)}, u32[]{:S(2)}) collective-permute-start(bf16[8,144,128]{2,1,0:T(8,128)(2,1)S(1)} %get-tuple-element.7), channel_id=1, source_target_pairs={{0,15},{1,0},{2,1},{3,2},{4,3},{5,4},{6,5},{7,6},{8,7},{9,8},{10,9... | collective-permute-start | bytes 884744 | tf_op jit(solution)/shard_map/ppermute | solution.py:167
  110.4 12.9 %collective-permute-start.1 = (bf16[8,144,128]{2,1,0:T(8,128)(2,1)S(1)}, bf16[8,144,128]{2,1,0:T(8,128)(2,1)S(1)}, u32[]{:S(2)}, u32[]{:S(2)}) collective-permute-start(bf16[8,144,128]{2,1,0:T(8,128)(2,1)S(1)} %get-tuple-element.9), channel_id=1, source_target_pairs={{0,1},{1,2},{2,3},{3,4},{4,5},{5,6},{6,7},{7,8},{8,9},{9,10},{10,1... | collective-permute-start | bytes 884744 | tf_op jit(solution)/shard_map/ppermute | solution.py:166
Sparse Core Ops, SparseCore 0:
  11.1 82.6 all-gather.1

commit v3 on v1

v3 whole, which is shorter than its diff:
```python
import functools

import jax
import jax.numpy as jnp
from jax import lax
from jax.experimental import pallas as pl
from jax.experimental.pallas import tpu as pltpu
from jax.sharding import PartitionSpec as P

OWN = 16
HALF = OWN // 2
CHUNK = 288
STEP = 16
UNROLL = 4
BF = jnp.bfloat16
F32 = jnp.float32


def left_kernel(rows, count, prolong, tiles, left, turned):
    step = pl.program_id(0)

    @pl.when(step == 0)
    def _():
        for r in range(prolong.shape[0]):
            turned[r] = prolong[r].T

    @pl.when(step * STEP < count[0])
    def _():
        for k in range(STEP):
            row = rows[step * STEP + k]
            left[k] = jnp.dot(turned[row], tiles[k], preferred_element_type=F32).astype(BF)


def left_products(rows, count, prolong, tiles):
    total, width, _ = tiles.shape

    def block(i, rows, count):
        return (jnp.minimum(i, (count[0] - 1) // STEP), 0, 0)

    return pl.pallas_call(
        left_kernel,
        grid_spec=pltpu.PrefetchScalarGridSpec(
            num_scalar_prefetch=2,
            grid=(total // STEP,),
            in_specs=[
                pl.BlockSpec(prolong.shape, lambda i, rows, count: (0, 0, 0)),
                pl.BlockSpec((STEP, width, width), block),
            ],
            out_specs=pl.BlockSpec((STEP, width, width), block),
            scratch_shapes=[pltpu.VMEM(prolong.shape, BF)],
        ),
        out_shape=jax.ShapeDtypeStruct(tiles.shape, BF),
        compiler_params=pltpu.CompilerParams(vmem_limit_bytes=32 << 20),
        cost_estimate=pl.CostEstimate(flops=2 * total * width**3, bytes_accessed=4 * total * width**2, transcendentals=0),
        name="left_products",
    )(rows, count, prolong, tiles)


def column_kernel(first, sources, kind, where, slot, group, count, parity, left, *rest):
    blocks, rest = rest[:sources], rest[sources:]
    if first:
        old_sums, old_feats, send, keep, held_l, held_b, sums, feats, order, sem_l, sem_b = rest
    else:
        sums, feats, held_l, held_b, order, sem_l, sem_b = rest
    live = count[0]
    spare_slot = sums.shape[0] - 1
    spare_group = feats.shape[0] // 128 - 1

    def choose(t, n):
        mine = (kind[t] >= first) & (kind[t] < first + sources)

        @pl.when(mine)
        def _():
            order[n] = t

        return n + mine.astype(jnp.int32)

    chosen = lax.fori_loop(0, live, choose, 0)
    turns = pl.cdiv(chosen, UNROLL)

    @pl.loop(chosen, turns * UNROLL)
    def _(n):
        order[n] = order[n - 1]

    @pl.loop(0, turns * UNROLL)
    def _(n):
        t = order[n]
        pltpu.make_async_copy(left.at[t], held_l.at[n], sem_l.at[n]).start()
        for k in range(sources):

            @pl.when(kind[t] == first + k)
            def _():
                pltpu.make_async_copy(blocks[k].at[where[t]], held_b.at[n], sem_b.at[n]).start()

    sums[...] = jnp.zeros_like(sums)
    feats[...] = jnp.zeros_like(feats)

    @pl.loop(0, turns)
    def _(i):
        for u in range(UNROLL):
            n = i * UNROLL + u
            pltpu.make_async_copy(left.at[0], held_l.at[n], sem_l.at[n]).wait()
            pltpu.make_async_copy(blocks[0].at[0], held_b.at[n], sem_b.at[n]).wait()
        for u in range(UNROLL):
            n = i * UNROLL + u
            t = order[n]
            both = jnp.dot(held_l[n], held_b[n], preferred_element_type=F32)
            s = jnp.where(n < chosen, slot[t], spare_slot)
            g = jnp.where(n < chosen, group[t], spare_group)
            rows = pl.ds(pl.multiple_of(g * 128, 128), 128)
            sums[s] += both[:, :128]
            feats[rows, :] += both[:, 128:]

    if not first:
        return
    p = parity[0]

    def put(ref, k, owner):
        for part in range(2):
            ref[k, 128 * part : 128 * part + 128] = (sums[2 * owner + part] + old_sums[2 * owner + part]).astype(ref.dtype)
        rows = pl.ds(pl.multiple_of(24 * owner, 8), 32)
        ref[k, 256:CHUNK] = (feats[rows, :] + old_feats[rows, :]).astype(ref.dtype)

    for k in range(HALF):
        put(send, k, 2 * k + 1 - p)
        put(keep, k, 2 * k + p)


def column_products(first, table, left, blocks, old=()):
    total = left.shape[0]
    smem = pl.BlockSpec(memory_space=pltpu.SMEM)
    vmem = pl.BlockSpec(memory_space=pltpu.VMEM)
    shape = (HALF, CHUNK, 128)
    held = [pltpu.VMEM((total, 128, 128), BF), pltpu.VMEM((total, 128, 256), BF)]
    sums = ((33, 128, 128), (4 * 128, 128))
    marks = [pltpu.SMEM((total + UNROLL,), jnp.int32), pltpu.SemaphoreType.DMA((total,)), pltpu.SemaphoreType.DMA((total,))]
    if first:
        outs = [jax.ShapeDtypeStruct(shape, t) for t in (BF, F32)]
        scratch = held + [pltpu.VMEM(s, F32) for s in sums] + marks
    else:
        outs = [jax.ShapeDtypeStruct(s, F32) for s in sums]
        scratch = held + marks
    return pl.pallas_call(
        functools.partial(column_kernel, first, len(blocks)),
        in_specs=[smem] * len(table) + [pl.BlockSpec(memory_space=pl.ANY)] * (1 + len(blocks)) + [vmem] * len(old),
        out_specs=[vmem] * len(outs),
        out_shape=outs,
        scratch_shapes=scratch,
        compiler_params=pltpu.CompilerParams(vmem_limit_bytes=48 << 20),
        cost_estimate=pl.CostEstimate(flops=2 * total * 128**3, bytes_accessed=6 << 20, transcendentals=0),
        name="column_products",
    )(*table, left, *blocks, *old)


def pair_kernel(keep, came, out):
    out[...] = (keep[...] + came[...].astype(F32)).astype(BF)


def pair_sums(keep, came):
    return pl.pallas_call(
        pair_kernel,
        out_shape=jax.ShapeDtypeStruct(keep.shape, BF),
        compiler_params=pltpu.CompilerParams(vmem_limit_bytes=16 << 20),
        name="pair_sums",
    )(keep, came)


def last_kernel(parts, tiles, feats):
    total = parts[0].astype(F32)
    for k in range(1, HALF):
        total += parts[k].astype(F32)
    tiles[0] = total[0:128]
    tiles[1] = total[128:256]
    feats[...] = total[256:280]


def last_sums(parts):
    return pl.pallas_call(
        last_kernel,
        out_shape=[jax.ShapeDtypeStruct((2, 128, 128), F32), jax.ShapeDtypeStruct((24, 128), F32)],
        compiler_params=pltpu.CompilerParams(vmem_limit_bytes=16 << 20),
        name="last_sums",
    )(parts)


def own_sums(send, keep):
    trade = []
    for d in range(32):
        for z in range(OWN):
            up = z % 2 == d % 2
            trade.append((d * OWN + z, d * OWN + (z + (1 if up else -1)) % OWN))
    mid = pair_sums(keep, lax.ppermute(send, ("dom", "own"), trade))
    groups = [[2 * k + b for k in range(HALF)] for b in range(2)]
    return last_sums(lax.all_to_all(mid, "own", 0, 0, tiled=True, axis_index_groups=groups))


def gather(pairs):
    over_x = [[[8 * y + 2 * x + c for x in range(4)] for y in range(4)] for c in range(2)]
    over_y = [[[8 * y + 2 * x + c for y in range(4)] for x in range(4)] for c in range(2)]
    for groups in (over_x[0] + over_y[1], over_y[0] + over_x[1]):
        pairs = lax.all_to_all(jnp.tile(pairs, (4, 1, 1)), "dom", 0, 0, tiled=True, axis_index_groups=groups)
    return pairs, lax.ppermute(pairs, "dom", [(i, i ^ 1) for i in range(32)])


def places(col_dom, col_local):
    y, x, core = col_dom // 8, col_dom // 2 % 4, col_dom % 2
    kind = jnp.where(core == lax.axis_index("dom") % 2, 0, 1)
    return kind, jnp.where(core == 0, y * 4 + x, x * 4 + y) * 6 + col_local


def local(tiles, prolong, features, match, row_local, col_dom, col_local, coarse_slot, tile_count):
    here, there = gather(jnp.concatenate([prolong, features], axis=2))
    left = left_products(row_local, tile_count, prolong, tiles)
    kind, where = places(col_dom[:, 0], col_local)
    parity = jnp.reshape(lax.axis_index("own") % 2, (1,)).astype(jnp.int32)
    table = (kind, where, coarse_slot, match[row_local], tile_count, parity)
    old = column_products(0, table, left, (here,))
    send, keep = column_products(1, table, left, (there,), old)
    return own_sums(send, keep)


def solution(mesh):
    placed = (
        P(("dom", "own"), None, None),
        P("dom", None, None),
        P("dom", None, None),
        P("dom"),
        P(("dom", "own")),
        P(("dom", "own"), None),
        P(("dom", "own")),
        P(("dom", "own")),
        P(("dom", "own")),
    )
    return jax.shard_map(
        local,
        mesh=mesh,
        in_specs=placed,
        out_specs=(P(("dom", "own"), None, None), P(("dom", "own"), None)),
        check_vma=False,
    )
```

time: 268 us -> 157 us (0.59)
  the two profiles are of different devices: /device:TPU:6 before, /device:TPU:1 now
where the time goes in v3:
time: 157 us; the launch traced here: 156 us
  blocking collectives  109 us (69%)
  starting transfers between devices  15.4 us (10%)
  Pallas kernels  14.5 us (9%)
  waiting for transfers between devices  7.26 us (5%)
  other arithmetic  4.9 us (3%)
  local copies, waits for them, and re-layouts  3.77 us (2%)
    all_to_all x2, blocking collectives, gather(): lax.all_to_all(jnp.tile(pairs, (4, 1, 1)), 'dom', 0, 0, tiled=True, axis_...  59.5 us
    all_to_all x1, blocking collectives, own_sums(): lax.all_to_all(mid, 'own', 0, 0, tiled=True, axis_index_groups=groups)  49.5 us
    pallas_call x2, Pallas kernels, column_products(): pl.pallas_call(functools.partial(column_kernel, first, len(blocks)), in_s...  11.8 us
    ppermute x1, starting transfers between devices, gather(): return (pairs, lax.ppermute(pairs, 'dom', [(i, i ^ 1) for i in range(32)]))  8.09 us
    ppermute x1, starting transfers between devices, own_sums(): mid = pair_sums(keep, lax.ppermute(send, ('dom', 'own'), trade))  7.28 us
    ppermute x1, waiting for transfers between devices, own_sums(): mid = pair_sums(keep, lax.ppermute(send, ('dom', 'own'), trade))  7.26 us
    gather x1, other arithmetic, local(): table = (kind, where, coarse_slot, match[row_local], tile_count, parity)  3.8 us
  transfers between devices with their start and end apart: 2, of which 1 were waited for; matrix products, arithmetic and copies ran while one was open for 3% of the time, Pallas kernels for 5%

profile of v3, /device:TPU:1, one launch (start us, length us, event | category | flops | bytes accessed | tf_op | source)
XLA Modules:
  0.0 156.3 jit_solution(2237946834959206095)
XLA Ops:
  0.6 1.1 pad_maximum_fusion
  1.7 0.2 tile.8
  1.9 17.7 %all_to_all.15 = bf16[24,128,256]{2,1,0:T(8,128)(2,1)S(1)} all-to-all(bf16[24,128,256]{2,1,0:T(8,128)(2,1)S(1)} %bitcast.30), channel_id=1, replica_groups={{0,32,64,96},{128,160,192,224},{256,288,320,352},{384,416,448,480},{16,..., dimensions={0} | all-to-all | bytes 3145728 | tf_op jit(solution)/shard_map/all_to_all | solution.py:201
  19.5 0.8 tile.20
  20.3 0.0 copy-start.2
  20.3 0.0 copy-start.4
  20.3 41.9 %all_to_all.16.rest_0_ = bf16[96,128,256]{2,1,0:T(8,128)(2,1)} all-to-all(bf16[96,128,256]{2,1,0:T(8,128)(2,1)S(1)} %bitcast.29), channel_id=1, replica_groups={{0,128,256,384},{32,160,288,416},{64,192,320,448},{96,224,352,480},{16,..., dimensions={0} | all-to-all | bytes 12582912 | tf_op jit(solution)/shard_map/all_to_all | solution.py:201
  62.2 8.1 %collective-permute-start = (bf16[96,128,256]{2,1,0:T(8,128)(2,1)}, bf16[96,128,256]{2,1,0:T(8,128)(2,1)}, u32[]{:S(2)}, u32[]{:S(2)}) collective-permute-start(bf16[96,128,256]{2,1,0:T(8,128)(2,1)} %all_to_all.16.rest_0_), channel_id=1, source_target_pairs={{0,16},{16,0},{32,48},{48,32},{64,80},{80,64},{96,112},{112,96},{1... | collective-permute-start | bytes 18874376 | tf_op jit(solution)/shard_map/ppermute | solution.py:202
  71.0 0.0 copy-done.2
  71.0 0.0 copy-done.4
  71.0 0.0 copy-start.1
  71.0 2.0 %copy-done.1 = bf16[112,128,128]{2,1,0:T(8,128)(2,1)S(1)} copy-done((bf16[112,128,128]{2,1,0:T(8,128)(2,1)S(1)}, bf16[112,128,128]{2,1,0:T(8,128)(2,1)}, u32[]{:S(2)}) %copy-start.1) | copy-done | bytes 3670040
  73.1 1.8 %left_products.1.left = bf16[112,128,128]{2,1,0:T(8,128)(2,1)S(1)} custom-call(s32[112]{0:T(128)S(1)} %copy-done.4, s32[1]{0:T(128)S(6)} %copy.11.count, bf16[6,128,128]{2,1,0:T(8,128)(2,1)S(1)} %copy-done.2, bf16[112,128,128]{2,1,0:T(8,128)(2,1)S(1)} %copy-done.1), custom_call_target="tpu_custom_call" | custom-call | flops 469762048 | bytes 7340032 | tf_op jit(solution)/shard_map/left_products/pallas_call | solution.py:40
  74.9 0.8 fusion.3
  75.6 3.8 %compare_select_fusion.3.group = s32[112]{0:T(128)S(1)} fusion(s32[112]{0:T(128)S(1)} %copy-done.4, s32[]{:T(128)} %bitcast.1, s32[]{:T(128)} %bitcast.2, s32[]{:T(128)} %bitcast.3, s32[]{:T(128)} %bitcast.4, s32[]{:T(128)} %bitcast.5, s32[]{:T(128)} %bitcast.6), kind=kLoop, calls=%fused_computation.4 | loop fusion | flops 1456 | bytes 920 | tf_op jit(solution)/shard_map/gather | solution.py:216
  79.5 6.0 %column_products.2 = (f32[33,128,128]{2,1,0:T(8,128)S(1)}, f32[512,128]{1,0:T(8,128)S(1)}) custom-call(s32[112]{0:T(128)S(1)} %get-tuple-element.17.kind, s32[112]{0:T(128)S(1)} %get-tuple-element.16.where, s32[112]{0:T(128)S(1)} %copy-done.3, s32[112]{0:T(128)S(1)} %compare_select_fusion.3.group, s32[1]{0:T(128)S(6)} %copy.11.count, s32[1]{0:T(128)} %bitcast.7.parity, ...), custom_call_target="tpu_custom_call" | custom-call | flops 469762048 | bytes 6291456 | tf_op jit(solution)/shard_map/column_products/pallas_call | solution.py:143
  85.5 0.0 copy-done
  85.5 0.0 collective-permute-done.rest_0_
  85.5 5.9 %column_products.3 = (bf16[8,288,128]{2,1,0:T(8,128)(2,1)S(1)}, f32[8,288,128]{2,1,0:T(8,128)S(1)}) custom-call(s32[112]{0:T(128)S(1)} %get-tuple-element.17.kind, s32[112]{0:T(128)S(1)} %get-tuple-element.16.where, s32[112]{0:T(128)S(1)} %copy-done.3, s32[112]{0:T(128)S(1)} %compare_select_fusion.3.group, s32[1]{0:T(128)S(6)} %copy.11.count, ...), custom_call_target="tpu_custom_call" | custom-call | flops 469762048 | bytes 6291456 | tf_op jit(solution)/shard_map/column_products/pallas_call | solution.py:143
  91.4 7.3 %collective-permute-start.1 = (bf16[8,288,128]{2,1,0:T(8,128)(2,1)S(1)}, bf16[8,288,128]{2,1,0:T(8,128)(2,1)S(1)}, u32[]{:S(2)}, u32[]{:S(2)}) collective-permute-start(bf16[8,288,128]{2,1,0:T(8,128)(2,1)S(1)} %get-tuple-element.9), channel_id=1, source_target_pairs={{0,1},{1,0},{2,3},{3,2},{4,5},{5,4},{6,7},{7,6},{8,9},{9,8},{10,11... | collective-permute-start | bytes 1769480 | tf_op jit(solution)/shard_map/ppermute | solution.py:192
  98.7 7.3 %collective-permute-done.1.came = bf16[8,288,128]{2,1,0:T(8,128)(2,1)S(1)} collective-permute-done((bf16[8,288,128]{2,1,0:T(8,128)(2,1)S(1)}, bf16[8,288,128]{2,1,0:T(8,128)(2,1)S(1)}, u32[]{:S(2)}, u32[]{:S(2)}) %collective-permute-start.1) | collective-permute-done | bytes 589856 | tf_op jit(solution)/shard_map/ppermute | solution.py:192
  105.9 0.1 pair_sums.1
  106.1 49.5 %all_to_all.17.parts = bf16[8,288,128]{2,1,0:T(8,128)(2,1)S(1)} all-to-all(bf16[8,288,128]{2,1,0:T(8,128)(2,1)S(1)} %pair_sums.1), channel_id=1, replica_groups={{0,2,4,6,8,10,12,14},{1,3,5,7,9,11,13,15},{16,18,20,22,24,26,28,30},{17..., dimensions={0} | all-to-all | bytes 1179648 | tf_op jit(solution)/shard_map/all_to_all | solution.py:194
  155.6 0.7 last_sums.1
  (10 shorter events, 0.0 us)
Async XLA Ops:
  20.3 50.7 %copy-start.2 = (bf16[6,128,128]{2,1,0:T(8,128)(2,1)S(1)}, bf16[6,128,128]{2,1,0:T(8,128)(2,1)}, u32[]{:S(2)}) copy-start(bf16[6,128,128]{2,1,0:T(8,128)(2,1)} %prolong.1) | copy-start | bytes 589828
  20.3 50.7 %copy-start.4 = (s32[112]{0:T(128)S(1)}, s32[112]{0:T(128)}, u32[]{:S(2)}) copy-start(s32[112]{0:T(128)} %rows.1) | copy-start | bytes 1348
  62.2 23.3 %collective-permute-start = (bf16[96,128,256]{2,1,0:T(8,128)(2,1)}, bf16[96,128,256]{2,1,0:T(8,128)(2,1)}, u32[]{:S(2)}, u32[]{:S(2)}) collective-permute-start(bf16[96,128,256]{2,1,0:T(8,128)(2,1)} %all_to_all.16.rest_0_), channel_id=1, source_target_pairs={{0,16},{16,0},{32,48},{48,32},{64,80},{80,64},{96,112},{112,96},{1... | collective-permute-start | bytes 18874376 | tf_op jit(solution)/shard_map/ppermute | solution.py:202
  71.0 2.0 %copy-start.1 = (bf16[112,128,128]{2,1,0:T(8,128)(2,1)S(1)}, bf16[112,128,128]{2,1,0:T(8,128)(2,1)}, u32[]{:S(2)}) copy-start(bf16[112,128,128]{2,1,0:T(8,128)(2,1)} %tiles.1) | copy-start | bytes 11010052
  73.0 1.8 %copy-start.5 = (s32[6]{0:T(128)S(1)}, s32[6]{0:T(128)}, u32[]{:S(2)}) copy-start(s32[6]{0:T(128)} %param.12) | copy-start | bytes 76
  73.1 6.4 %copy-start.6 = (s32[112]{0:T(128)S(1)}, s32[112]{0:T(128)}, u32[]{:S(2)}) copy-start(s32[112]{0:T(128)} %param.15) | copy-start | bytes 1348
  73.1 6.4 %copy-start.7 = (s32[112,1]{0,1:T(1,128)S(1)}, s32[112,1]{0,1:T(1,128)}, u32[]{:S(2)}) copy-start(s32[112,1]{0,1:T(1,128)} %param.14) | copy-start | bytes 1348
  73.1 6.4 %copy-start.3 = (s32[112]{0:T(128)S(1)}, s32[112]{0:T(128)}, u32[]{:S(2)}) copy-start(s32[112]{0:T(128)} %slot.3) | copy-start | bytes 1348
  74.8 10.6 %copy-start = (bf16[112,128,128]{2,1,0:T(8,128)(2,1)}, bf16[112,128,128]{2,1,0:T(8,128)(2,1)S(1)}, u32[]{:S(2)}) copy-start(bf16[112,128,128]{2,1,0:T(8,128)(2,1)S(1)} %left_products.1.left) | copy-start | bytes 11010052
  91.4 14.5 %collective-permute-start.1 = (bf16[8,288,128]{2,1,0:T(8,128)(2,1)S(1)}, bf16[8,288,128]{2,1,0:T(8,128)(2,1)S(1)}, u32[]{:S(2)}, u32[]{:S(2)}) collective-permute-start(bf16[8,288,128]{2,1,0:T(8,128)(2,1)S(1)} %get-tuple-element.9), channel_id=1, source_target_pairs={{0,1},{1,0},{2,3},{3,2},{4,5},{5,4},{6,7},{7,6},{8,9},{9,8},{10,11... | collective-permute-start | bytes 1769480 | tf_op jit(solution)/shard_map/ppermute | solution.py:192

commit v4 on v3

v4 whole, which is shorter than its diff:
```python
import jax
import jax.numpy as jnp
from jax import lax
from jax.experimental import pallas as pl
from jax.experimental.pallas import tpu as pltpu
from jax.sharding import PartitionSpec as P

OWN = 16
BD = 6
TD = 112
PLAN = 256
SPARE = 64
HALF = OWN // 2
CHUNK = 288
STEP = 16
UNROLL = 8
BF = jnp.bfloat16
F32 = jnp.float32


def copies_kernel(prolong, features, copies, held, sems):
    moves = [pltpu.make_async_copy(ref, held.at[k], sems.at[k]) for k, ref in enumerate((prolong, features))]
    for move in moves:
        move.start()
    for move in moves:
        move.wait()
    for k in range(4):
        for r in range(BD):
            copies[k * BD + r, :, 0:128] = held[0, r]
            copies[k * BD + r, :, 128:256] = held[1, r]


def four_copies(prolong, features):
    return pl.pallas_call(
        copies_kernel,
        in_specs=[pl.BlockSpec(memory_space=pltpu.HBM)] * 2,
        out_specs=pl.BlockSpec(memory_space=pltpu.VMEM),
        out_shape=jax.ShapeDtypeStruct((4 * BD, 128, 256), BF),
        scratch_shapes=[pltpu.VMEM((2,) + prolong.shape, BF), pltpu.SemaphoreType.DMA((2,))],
        compiler_params=pltpu.CompilerParams(vmem_limit_bytes=16 << 20),
        name="four_copies",
    )(prolong, features)


def left_kernel(rows, count, prolong, tiles, after, left, turned):
    step = pl.program_id(0)

    @pl.when(step == 0)
    def _():
        for r in range(BD):
            turned[r] = prolong[r].T

    @pl.when(step * STEP < count[0])
    def _():
        for k in range(STEP):
            row = rows[step * STEP + k]
            left[k] = jnp.dot(turned[row], tiles[k], preferred_element_type=F32).astype(BF)


def left_products(rows, count, prolong, tiles, after):
    total, width, _ = tiles.shape

    def block(i, rows, count):
        return (jnp.minimum(i, (count[0] - 1) // STEP), 0, 0)

    return pl.pallas_call(
        left_kernel,
        grid_spec=pltpu.PrefetchScalarGridSpec(
            num_scalar_prefetch=2,
            grid=(total // STEP,),
            in_specs=[pl.BlockSpec(prolong.shape, lambda i, rows, count: (0, 0, 0)), pl.BlockSpec((STEP, width, width), block), pl.BlockSpec(memory_space=pl.ANY)],
            out_specs=pl.BlockSpec((STEP, width, width), block),
            scratch_shapes=[pltpu.VMEM(prolong.shape, BF)],
        ),
        out_shape=jax.ShapeDtypeStruct(tiles.shape, BF),
        compiler_params=pltpu.CompilerParams(vmem_limit_bytes=48 << 20),
        cost_estimate=pl.CostEstimate(flops=2 * total * width**3, bytes_accessed=4 * total * width**2, transcendentals=0),
        name="left_products",
    )(rows, count, prolong, tiles, after)


def plan_kernel(place, mine, theirs, plan):
    start = place[0] * 96
    chosen = jnp.int32(0)
    for d, table in enumerate((mine, theirs)):

        def choose(t, n):
            at = table[0, t] - start
            plan[0, n] = d * TD + t
            plan[1, n] = jnp.clip(at, 0, 95)
            plan[2, n] = d * 32 + table[1, t]
            plan[3, n] = (d * 3 + table[3, table[2, t]]) * 128
            return n + ((at >= 0) & (at < 96)).astype(jnp.int32)

        chosen = lax.fori_loop(0, table[3, BD], choose, chosen)

    @pl.loop(chosen, chosen + UNROLL)
    def _(n):
        plan[0, n] = 0
        plan[1, n] = 0
        plan[2, n] = SPARE
        plan[3, n] = 6 * 128

    plan[0, PLAN - 1] = chosen
    plan[1, PLAN - 1] = mine[3, BD]
    plan[2, PLAN - 1] = theirs[3, BD]


def plan_products(place, mine, theirs):
    smem = pl.BlockSpec(memory_space=pltpu.SMEM)
    return pl.pallas_call(
        plan_kernel,
        in_specs=[smem] * 3,
        out_specs=smem,
        out_shape=jax.ShapeDtypeStruct((4, PLAN), jnp.int32),
        name="plan_products",
    )(place, mine, theirs)


def column_kernel(plan, left, left_theirs, blocks, keep, give, held_l, held_b, sums, feats, sems):
    moves = []
    for d, ref in enumerate((left, left_theirs)):
        for i in range(TD // STEP):
            move = pltpu.make_async_copy(ref.at[pl.ds(i * STEP, STEP)], held_l.at[pl.ds(d * TD + i * STEP, STEP)], sems.at[len(moves)])
            moves.append((i * STEP < plan[1 + d, PLAN - 1], move))
    moves.append((True, pltpu.make_async_copy(blocks, held_b, sems.at[len(moves)])))
    for live, move in moves:
        pl.when(live)(move.start)
    sums[...] = jnp.zeros_like(sums)
    feats[...] = jnp.zeros_like(feats)
    for live, move in moves:
        pl.when(live)(move.wait)

    @pl.loop(0, pl.cdiv(plan[0, PLAN - 1], UNROLL))
    def _(i):
        for u in range(UNROLL):
            n = i * UNROLL + u
            both = jnp.dot(held_l[plan[0, n]], held_b[plan[1, n]], preferred_element_type=F32)
            rows = pl.ds(pl.multiple_of(plan[3, n], 128), 128)
            sums[plan[2, n]] += both[:, :128]
            feats[rows, :] += both[:, 128:]

    for d, ref in enumerate((keep, give)):
        for o in range(OWN):
            for part in range(2):
                ref[o, 128 * part : 128 * part + 128] = sums[32 * d + 2 * o + part].astype(ref.dtype)
            ref[o, 256:CHUNK] = feats[384 * d + 24 * o : 384 * d + 24 * o + 32, :].astype(ref.dtype)


def column_products(plan, left, left_theirs, blocks):
    vmem = pl.BlockSpec(memory_space=pltpu.VMEM)
    return pl.pallas_call(
        column_kernel,
        in_specs=[pl.BlockSpec(memory_space=pltpu.SMEM)] + [pl.BlockSpec(memory_space=pltpu.HBM)] * 3,
        out_specs=[vmem] * 2,
        out_shape=[jax.ShapeDtypeStruct((OWN, CHUNK, 128), t) for t in (F32, BF)],
        scratch_shapes=[
            pltpu.VMEM((2 * TD, 128, 128), BF),
            pltpu.VMEM(blocks.shape, BF),
            pltpu.VMEM((SPARE + 1, 128, 128), F32),
            pltpu.VMEM((7 * 128, 128), F32),
            pltpu.SemaphoreType.DMA((2 * TD // STEP + 1,)),
        ],
        compiler_params=pltpu.CompilerParams(vmem_limit_bytes=40 << 20),
        cost_estimate=pl.CostEstimate(flops=4 * TD * 128**3, bytes_accessed=18 << 20, transcendentals=0),
        name="column_products",
    )(plan, left, left_theirs, blocks)


def fold_kernel(place, keep, came, stay, send):
    p = place[1]
    for k in range(HALF):
        here, there = 2 * k + p, 2 * k + 1 - p
        stay[k] = keep[here] + came[here].astype(F32)
        send[k] = (keep[there] + came[there].astype(F32)).astype(BF)


def fold_sums(place, keep, came):
    vmem = pl.BlockSpec(memory_space=pltpu.VMEM)
    return pl.pallas_call(
        fold_kernel,
        in_specs=[pl.BlockSpec(memory_space=pltpu.SMEM), vmem, vmem],
        out_specs=[vmem] * 2,
        out_shape=[jax.ShapeDtypeStruct((HALF, CHUNK, 128), t) for t in (F32, BF)],
        compiler_params=pltpu.CompilerParams(vmem_limit_bytes=24 << 20),
        name="fold_sums",
    )(place, keep, came)


def pair_kernel(keep, came, out):
    out[...] = (keep[...] + came[...].astype(F32)).astype(BF)


def pair_sums(keep, came):
    return pl.pallas_call(
        pair_kernel,
        out_shape=jax.ShapeDtypeStruct(keep.shape, BF),
        compiler_params=pltpu.CompilerParams(vmem_limit_bytes=16 << 20),
        name="pair_sums",
    )(keep, came)


def last_kernel(parts, tiles, feats):
    total = parts[0].astype(F32)
    for k in range(1, HALF):
        total += parts[k].astype(F32)
    tiles[0] = total[0:128]
    tiles[1] = total[128:256]
    feats[...] = total[256:280]


def last_sums(parts):
    return pl.pallas_call(
        last_kernel,
        out_shape=[jax.ShapeDtypeStruct((2, 128, 128), F32), jax.ShapeDtypeStruct((24, 128), F32)],
        compiler_params=pltpu.CompilerParams(vmem_limit_bytes=16 << 20),
        name="last_sums",
    )(parts)


def own_sums(send, keep):
    trade = []
    for d in range(32):
        for z in range(OWN):
            up = z % 2 == d % 2
            trade.append((d * OWN + z, d * OWN + (z + (1 if up else -1)) % OWN))
    mid = pair_sums(keep, lax.ppermute(send, ("dom", "own"), trade))
    groups = [[2 * k + b for k in range(HALF)] for b in range(2)]
    return last_sums(lax.all_to_all(mid, "own", 0, 0, tiled=True, axis_index_groups=groups))


def gather(copies):
    over_x = [[[8 * y + 2 * x + c for x in range(4)] for y in range(4)] for c in range(2)]
    over_y = [[[8 * y + 2 * x + c for y in range(4)] for x in range(4)] for c in range(2)]
    nearby = lax.all_to_all(copies, "dom", 0, 0, tiled=True, axis_index_groups=over_x[0] + over_y[1])
    copies = jnp.tile(nearby, (4, 1, 1))
    return lax.all_to_all(copies, "dom", 0, 0, tiled=True, axis_index_groups=over_y[0] + over_x[1])


def places(col_dom, col_local):
    y, x, core = col_dom // 8, col_dom // 2 % 4, col_dom % 2
    return 96 * core + jnp.where(core == 0, y * 4 + x, x * 4 + y) * BD + col_local


def local(tiles, prolong, features, match, row_local, col_dom, col_local, coarse_slot, tile_count):
    copies = four_copies(prolong, features)
    left = left_products(row_local, tile_count, prolong, tiles, copies)
    last = jnp.concatenate([match, tile_count, jnp.zeros((tiles.shape[0] - BD - 1,), jnp.int32)])
    mine = jnp.stack([places(col_dom[:, 0], col_local), coarse_slot, row_local, last])
    swap = [(i, i ^ 1) for i in range(32)]
    theirs, left_theirs = lax.ppermute(mine, "dom", swap), lax.ppermute(left, "dom", swap)
    blocks = gather(copies)
    place = jnp.stack([lax.axis_index("dom") % 2, lax.axis_index("own") % 2]).astype(jnp.int32)
    plan = plan_products(place, mine, theirs)
    keep, give = column_products(plan, left, left_theirs, blocks)
    stay, send = fold_sums(place, keep, lax.ppermute(give, "dom", swap))
    return own_sums(send, stay)


def solution(mesh):
    placed = (
        P(("dom", "own"), None, None),
        P("dom", None, None),
        P("dom", None, None),
        P("dom"),
        P(("dom", "own")),
        P(("dom", "own"), None),
        P(("dom", "own")),
        P(("dom", "own")),
        P(("dom", "own")),
    )
    return jax.shard_map(
        local,
        mesh=mesh,
        in_specs=placed,
        out_specs=(P(("dom", "own"), None, None), P(("dom", "own"), None)),
        check_vma=False,
    )
```

time: 157 us -> 146 us (0.930)
  the two profiles are of different devices: /device:TPU:1 before, /device:TPU:6 now
where the time goes in v4:
time: 146 us
  blocking collectives  69.9 us (48%)
  waiting for transfers between devices  38.1 us (26%)
  Pallas kernels  15.2 us (10%)
  starting transfers between devices  13.6 us (9%)
  local copies, waits for them, and re-layouts  6.57 us (4%)
  between operations  1.48 us (1%)
    all_to_all x1, blocking collectives, own_sums(): lax.all_to_all(mid, 'own', 0, 0, tiled=True, axis_index_groups=groups)  50 us
    all_to_all x1, waiting for transfers between devices, gather(): lax.all_to_all(copies, 'dom', 0, 0, tiled=True, axis_index_groups=over_y[...  22.3 us
    all_to_all x1, blocking collectives, gather(): lax.all_to_all(copies, 'dom', 0, 0, tiled=True, axis_index_groups=over_x[...  19.9 us
    ppermute x1, waiting for transfers between devices, own_sums(): mid = pair_sums(keep, lax.ppermute(send, ('dom', 'own'), trade))  9.85 us
    pallas_call x1, Pallas kernels, column_products(): pl.pallas_call(column_kernel, in_specs=[pl.BlockSpec(memory_space=pltpu.S...  5.82 us
    all_to_all x1, starting transfers between devices, gather(): lax.all_to_all(copies, 'dom', 0, 0, tiled=True, axis_index_groups=over_y[...  5.39 us
    pallas_call x1, Pallas kernels, left_products(): pl.pallas_call(left_kernel, grid_spec=pltpu.PrefetchScalarGridSpec(num_sc...  4.61 us
    another operation x1, local copies, waits for them, and re-layouts, gather(): copies = jnp.tile(nearby, (4, 1, 1))  3.39 us
  transfers between devices with their start and end apart: 5, of which 4 were waited for; matrix products, arithmetic and copies ran while one was open for 0% of the time, Pallas kernels for 5%

profile of v4, /device:TPU:6, one launch (start us, length us, event | category | flops | bytes accessed | tf_op | source)
XLA Modules:
  0.0 145.6 jit_solution(3342338240018288884)
XLA Ops:
  0.6 0.9 copy-done
  1.6 0.9 copy-done.2
  2.5 0.7 four_copies.1.after
  3.2 19.9 %all_to_all.15 = bf16[24,128,256]{2,1,0:T(8,128)(2,1)S(1)} all-to-all(bf16[24,128,256]{2,1,0:T(8,128)(2,1)S(1)} %four_copies.1.after), channel_id=1, replica_groups={{0,32,64,96},{128,160,192,224},{256,288,320,352},{384,416,448,480},{16,..., dimensions={0} | all-to-all | bytes 3145728 | tf_op jit(solution)/shard_map/all_to_all | solution.py:235
  23.1 3.4 %tile.4 = bf16[4,24,128,256]{3,2,1,0:T(8,128)(2,1)} broadcast(bf16[24,128,256]{2,1,0:T(8,128)(2,1)S(1)} %all_to_all.15), dimensions={1,2,3} | broadcast | bytes 7864320 | tf_op jit(solution)/shard_map/tile | solution.py:236
  26.5 5.4 %all-to-all-start.1 = ((bf16[96,128,256]{2,1,0:T(8,128)(2,1)}), bf16[96,128,256]{2,1,0:T(8,128)(2,1)}, u32[]{:S(2)}, u32[]{:S(2)}) async-start(bf16[96,128,256]{2,1,0:T(8,128)(2,1)} %bitcast.28), calls=%async_computation.1 | async-start | bytes 12582912 | tf_op jit(solution)/shard_map/all_to_all | solution.py:237
  32.6 4.6 %left_products.1.left = bf16[112,128,128]{2,1,0:T(8,128)(2,1)} custom-call(s32[112]{0:T(128)S(1)} %copy-done.4, s32[1]{0:T(128)S(6)} %copy.11.count, bf16[6,128,128]{2,1,0:T(8,128)(2,1)S(1)} %copy-done.1, bf16[112,128,128]{2,1,0:T(8,128)(2,1)} %tiles.1, bf16[24,128,256]{2,1,0:T(8,128)(2,1)S(1)} %four_copies.1.after), custom_call_target="tpu_custom_call" | custom-call | flops 469762048 | bytes 7340032 | tf_op jit(solution)/shard_map/left_products/pallas_call | solution.py:66
  37.2 1.9 %collective-permute-start.1 = (bf16[112,128,128]{2,1,0:T(8,128)(2,1)}, bf16[112,128,128]{2,1,0:T(8,128)(2,1)}, u32[]{:S(2)}, u32[]{:S(2)}) collective-permute-start(bf16[112,128,128]{2,1,0:T(8,128)(2,1)} %left_products.1.left), channel_id=1, source_target_pairs={{0,16},{16,0},{32,48},{48,32},{64,80},{80,64},{96,112},{112,96},{1... | collective-permute-start | bytes 11010056 | tf_op jit(solution)/shard_map/ppermute | solution.py:251
  39.3 2.4 %collective-permute-start = (s32[4,112]{1,0:T(4,128)S(1)}, s32[4,112]{1,0:T(4,128)S(1)}, u32[]{:S(2)}, u32[]{:S(2)}) collective-permute-start(s32[4,112]{1,0:T(4,128)S(1)} %pad_add_fusion.mine), channel_id=1, source_target_pairs={{0,16},{16,0},{32,48},{48,32},{64,80},{80,64},{96,112},{112,96},{1... | collective-permute-start | bytes 5384 | tf_op jit(solution)/shard_map/ppermute | solution.py:251
  41.8 0.6 pad_add_fusion.1.place
  42.4 3.2 %collective-permute-done.theirs = s32[4,112]{1,0:T(4,128)S(1)} collective-permute-done((s32[4,112]{1,0:T(4,128)S(1)}, s32[4,112]{1,0:T(4,128)S(1)}, u32[]{:S(2)}, u32[]{:S(2)}) %collective-permute-start) | collective-permute-done | bytes 1824 | tf_op jit(solution)/shard_map/ppermute | solution.py:251
  45.5 0.6 copy-done.7
  46.1 2.5 %plan_products.1.plan = s32[4,256]{1,0:T(4,128)} custom-call(s32[2]{0:T(128)} %pad_add_fusion.1.place, s32[4,112]{1,0:T(4,128)} %copy-done.6, s32[4,112]{1,0:T(4,128)} %copy-done.7), custom_call_target="tpu_custom_call" | custom-call | tf_op jit(solution)/shard_map/plan_products/pallas_call | solution.py:111
  48.7 22.3 %all-to-all-done.1.blocks = bf16[96,128,256]{2,1,0:T(8,128)(2,1)} async-done(((bf16[96,128,256]{2,1,0:T(8,128)(2,1)}), bf16[96,128,256]{2,1,0:T(8,128)(2,1)}, u32[]{:S(2)}, u32[]{:S(2)}) %all-to-all-start.1) | async-done | bytes 6291488 | tf_op jit(solution)/shard_map/all_to_all | solution.py:237
  71.0 0.7 copy-done.3
  71.6 5.8 %column_products.1 = (f32[16,288,128]{2,1,0:T(8,128)S(1)}, bf16[16,288,128]{2,1,0:T(8,128)(2,1)S(1)}) custom-call(s32[4,256]{1,0:T(4,128)S(1)} %copy-done.3, bf16[112,128,128]{2,1,0:T(8,128)(2,1)} %left_products.1.left, bf16[112,128,128]{2,1,0:T(8,128)(2,1)} %collective-permute-done.1.left_theirs, bf16[96,128,256]{2,1,0:T(8,128)(2,1)} %all-to-all-done.1.blocks), custom_call_target="tpu_custom_call" | custom-call | flops 939524096 | bytes 18874368 | tf_op jit(solution)/shard_map/column_products/pallas_call | solution.py:152
  77.5 1.9 %collective-permute-start.2 = (bf16[16,288,128]{2,1,0:T(8,128)(2,1)S(1)}, bf16[16,288,128]{2,1,0:T(8,128)(2,1)S(1)}, u32[]{:S(2)}, u32[]{:S(2)}) collective-permute-start(bf16[16,288,128]{2,1,0:T(8,128)(2,1)S(1)} %get-tuple-element.7), channel_id=1, source_target_pairs={{0,16},{16,0},{32,48},{48,32},{64,80},{80,64},{96,112},{112,96},{1... | collective-permute-start | bytes 3538952 | tf_op jit(solution)/shard_map/ppermute | solution.py:256
  79.4 2.8 %collective-permute-done.2.came = bf16[16,288,128]{2,1,0:T(8,128)(2,1)S(1)} collective-permute-done((bf16[16,288,128]{2,1,0:T(8,128)(2,1)S(1)}, bf16[16,288,128]{2,1,0:T(8,128)(2,1)S(1)}, u32[]{:S(2)}, u32[]{:S(2)}) %collective-permute-start.2) | collective-permute-done | bytes 1179680 | tf_op jit(solution)/shard_map/ppermute | solution.py:256
  82.2 0.8 fold_sums.1
  83.0 1.9 %collective-permute-start.3 = (bf16[8,288,128]{2,1,0:T(8,128)(2,1)S(1)}, bf16[8,288,128]{2,1,0:T(8,128)(2,1)S(1)}, u32[]{:S(2)}, u32[]{:S(2)}) collective-permute-start(bf16[8,288,128]{2,1,0:T(8,128)(2,1)S(1)} %get-tuple-element.9), channel_id=1, source_target_pairs={{0,1},{1,0},{2,3},{3,2},{4,5},{5,4},{6,7},{7,6},{8,9},{9,8},{10,11... | collective-permute-start | bytes 1769480 | tf_op jit(solution)/shard_map/ppermute | solution.py:227
  84.9 9.8 %collective-permute-done.3.came = bf16[8,288,128]{2,1,0:T(8,128)(2,1)S(1)} collective-permute-done((bf16[8,288,128]{2,1,0:T(8,128)(2,1)S(1)}, bf16[8,288,128]{2,1,0:T(8,128)(2,1)S(1)}, u32[]{:S(2)}, u32[]{:S(2)}) %collective-permute-start.3) | collective-permute-done | bytes 589856 | tf_op jit(solution)/shard_map/ppermute | solution.py:227
  94.8 0.1 pair_sums.1
  94.9 50.0 %all_to_all.16.parts = bf16[8,288,128]{2,1,0:T(8,128)(2,1)S(1)} all-to-all(bf16[8,288,128]{2,1,0:T(8,128)(2,1)S(1)} %pair_sums.1), channel_id=1, replica_groups={{0,2,4,6,8,10,12,14},{1,3,5,7,9,11,13,15},{16,18,20,22,24,26,28,30},{17..., dimensions={0} | all-to-all | bytes 1179648 | tf_op jit(solution)/shard_map/all_to_all | solution.py:229
  144.8 0.7 last_sums.1
  (25 shorter events, 0.2 us)
Async XLA Ops:
  0.6 0.9 copy-start
  1.6 0.9 copy-start.2
  26.5 6.1 %copy-start.1 = (bf16[6,128,128]{2,1,0:T(8,128)(2,1)S(1)}, bf16[6,128,128]{2,1,0:T(8,128)(2,1)}, u32[]{:S(2)}) copy-start(bf16[6,128,128]{2,1,0:T(8,128)(2,1)} %prolong.3) | copy-start | bytes 589828
  26.5 6.1 %copy-start.4 = (s32[112]{0:T(128)S(1)}, s32[112]{0:T(128)}, u32[]{:S(2)}) copy-start(s32[112]{0:T(128)} %rows.1) | copy-start | bytes 1348
  26.5 44.4 %all-to-all-start.1 = ((bf16[96,128,256]{2,1,0:T(8,128)(2,1)}), bf16[96,128,256]{2,1,0:T(8,128)(2,1)}, u32[]{:S(2)}, u32[]{:S(2)}) async-start(bf16[96,128,256]{2,1,0:T(8,128)(2,1)} %bitcast.28), calls=%async_computation.1 | async-start | bytes 12582912 | tf_op jit(solution)/shard_map/all_to_all | solution.py:237
  32.6 6.6 %copy-start.8 = (s32[6]{0:T(128)S(1)}, s32[6]{0:T(128)}, u32[]{:S(2)}) copy-start(s32[6]{0:T(128)} %param.12) | copy-start | bytes 76
  32.6 6.7 %copy-start.10 = (s32[112]{0:T(128)S(1)}, s32[112]{0:T(128)}, u32[]{:S(2)}) copy-start(s32[112]{0:T(128)} %param.15) | copy-start | bytes 1348
  32.6 6.7 %copy-start.11 = (s32[112,1]{0,1:T(1,128)S(1)}, s32[112,1]{0,1:T(1,128)}, u32[]{:S(2)}) copy-start(s32[112,1]{0,1:T(1,128)} %param.14) | copy-start | bytes 1348
  32.6 6.7 %copy-start.9 = (s32[112]{0:T(128)S(1)}, s32[112]{0:T(128)}, u32[]{:S(2)}) copy-start(s32[112]{0:T(128)} %param.16) | copy-start | bytes 1348
  37.2 11.4 %collective-permute-start.1 = (bf16[112,128,128]{2,1,0:T(8,128)(2,1)}, bf16[112,128,128]{2,1,0:T(8,128)(2,1)}, u32[]{:S(2)}, u32[]{:S(2)}) collective-permute-start(bf16[112,128,128]{2,1,0:T(8,128)(2,1)} %left_products.1.left), channel_id=1, source_target_pairs={{0,16},{16,0},{32,48},{48,32},{64,80},{80,64},{96,112},{112,96},{1... | collective-permute-start | bytes 11010056 | tf_op jit(solution)/shard_map/ppermute | solution.py:251
  39.3 6.2 %copy-start.6 = (s32[4,112]{1,0:T(4,128)}, s32[4,112]{1,0:T(4,128)S(1)}, u32[]{:S(2)}) copy-start(s32[4,112]{1,0:T(4,128)S(1)} %pad_add_fusion.mine) | copy-start | bytes 5380
  39.3 6.2 %collective-permute-start = (s32[4,112]{1,0:T(4,128)S(1)}, s32[4,112]{1,0:T(4,128)S(1)}, u32[]{:S(2)}, u32[]{:S(2)}) collective-permute-start(s32[4,112]{1,0:T(4,128)S(1)} %pad_add_fusion.mine), channel_id=1, source_target_pairs={{0,16},{16,0},{32,48},{48,32},{64,80},{80,64},{96,112},{112,96},{1... | collective-permute-start | bytes 5384 | tf_op jit(solution)/shard_map/ppermute | solution.py:251
  45.5 0.6 copy-start.7
  46.1 36.1 %copy-start.5 = (s32[2]{0:T(128)S(1)}, s32[2]{0:T(128)}, u32[]{:S(2)}) copy-start(s32[2]{0:T(128)} %pad_add_fusion.1.place) | copy-start | bytes 28
  71.0 0.7 copy-start.3
  77.5 4.7 %collective-permute-start.2 = (bf16[16,288,128]{2,1,0:T(8,128)(2,1)S(1)}, bf16[16,288,128]{2,1,0:T(8,128)(2,1)S(1)}, u32[]{:S(2)}, u32[]{:S(2)}) collective-permute-start(bf16[16,288,128]{2,1,0:T(8,128)(2,1)S(1)} %get-tuple-element.7), channel_id=1, source_target_pairs={{0,16},{16,0},{32,48},{48,32},{64,80},{80,64},{96,112},{112,96},{1... | collective-permute-start | bytes 3538952 | tf_op jit(solution)/shard_map/ppermute | solution.py:256
  83.0 11.8 %collective-permute-start.3 = (bf16[8,288,128]{2,1,0:T(8,128)(2,1)S(1)}, bf16[8,288,128]{2,1,0:T(8,128)(2,1)S(1)}, u32[]{:S(2)}, u32[]{:S(2)}) collective-permute-start(bf16[8,288,128]{2,1,0:T(8,128)(2,1)S(1)} %get-tuple-element.9), channel_id=1, source_target_pairs={{0,1},{1,0},{2,3},{3,2},{4,5},{5,4},{6,7},{7,6},{8,9},{9,8},{10,11... | collective-permute-start | bytes 1769480 | tf_op jit(solution)/shard_map/ppermute | solution.py:227

commit v5 on v4

--- a/solution.py
+++ b/solution.py
@@ -13,33 +13,10 @@
 HALF = OWN // 2
 CHUNK = 288
 STEP = 16
-UNROLL = 8
+UNROLL = 16
 BF = jnp.bfloat16
+ORDER = [[[0, 1, 2, 3, 4, 5, 6, 7], [4, 5, 6, 7, 0, 1, 2, 3]], [[4, 5, 6, 7, 0, 1, 2, 3], [0, 1, 2, 3, 4, 5, 6, 7]]]
 F32 = jnp.float32
-
-
-def copies_kernel(prolong, features, copies, held, sems):
-    moves = [pltpu.make_async_copy(ref, held.at[k], sems.at[k]) for k, ref in enumerate((prolong, features))]
-    for move in moves:
-        move.start()
-    for move in moves:
-        move.wait()
-    for k in range(4):
-        for r in range(BD):
-            copies[k * BD + r, :, 0:128] = held[0, r]
-            copies[k * BD + r, :, 128:256] = held[1, r]
-
-
-def four_copies(prolong, features):
-    return pl.pallas_call(
-        copies_kernel,
-        in_specs=[pl.BlockSpec(memory_space=pltpu.HBM)] * 2,
-        out_specs=pl.BlockSpec(memory_space=pltpu.VMEM),
-        out_shape=jax.ShapeDtypeStruct((4 * BD, 128, 256), BF),
-        scratch_shapes=[pltpu.VMEM((2,) + prolong.shape, BF), pltpu.SemaphoreType.DMA((2,))],
-        compiler_params=pltpu.CompilerParams(vmem_limit_bytes=16 << 20),
-        name="four_copies",
-    )(prolong, features)
 
 
 def left_kernel(rows, count, prolong, tiles, after, left, turned):
@@ -79,6 +56,24 @@
     )(rows, count, prolong, tiles, after)
 
 
+def again_kernel(nearby, out):
+    out[0] = nearby[...]
+
+
+def four_times(nearby):
+    each = nearby.shape[0]
+    out = pl.pallas_call(
+        again_kernel,
+        grid=(2, 4),
+        in_specs=[pl.BlockSpec((each // 2,) + nearby.shape[1:], lambda i, k: (i, 0, 0))],
+        out_specs=pl.BlockSpec((1, each // 2) + nearby.shape[1:], lambda i, k: (k, i, 0, 0)),
+        out_shape=jax.ShapeDtypeStruct((4,) + nearby.shape, BF),
+        compiler_params=pltpu.CompilerParams(vmem_limit_bytes=16 << 20),
+        name="four_times",
+    )(nearby)
+    return out.reshape((4 * each,) + nearby.shape[1:])
+
+
 def plan_kernel(place, mine, theirs, plan):
     start = place[0] * 96
     chosen = jnp.int32(0)
@@ -117,19 +112,24 @@
     )(place, mine, theirs)
 
 
-def column_kernel(plan, left, left_theirs, blocks, keep, give, held_l, held_b, sums, feats, sems):
+def column_kernel(planned, left, left_theirs, blocks, keep, give, plan, held_l, held_b, sums, feats, sems):
+    table = pltpu.make_async_copy(planned, plan, sems.at[0])
+    table.start()
+    whole = pltpu.make_async_copy(blocks, held_b, sems.at[1])
+    whole.start()
+    table.wait()
     moves = []
     for d, ref in enumerate((left, left_theirs)):
         for i in range(TD // STEP):
-            move = pltpu.make_async_copy(ref.at[pl.ds(i * STEP, STEP)], held_l.at[pl.ds(d * TD + i * STEP, STEP)], sems.at[len(moves)])
+            move = pltpu.make_async_copy(ref.at[pl.ds(i * STEP, STEP)], held_l.at[pl.ds(d * TD + i * STEP, STEP)], sems.at[2 + len(moves)])
             moves.append((i * STEP < plan[1 + d, PLAN - 1], move))
-    moves.append((True, pltpu.make_async_copy(blocks, held_b, sems.at[len(moves)])))
     for live, move in moves:
         pl.when(live)(move.start)
     sums[...] = jnp.zeros_like(sums)
     feats[...] = jnp.zeros_like(feats)
     for live, move in moves:
         pl.when(live)(move.wait)
+    whole.wait()
 
     @pl.loop(0, pl.cdiv(plan[0, PLAN - 1], UNROLL))
     def _(i):
@@ -151,15 +151,16 @@
     vmem = pl.BlockSpec(memory_space=pltpu.VMEM)
     return pl.pallas_call(
         column_kernel,
-        in_specs=[pl.BlockSpec(memory_space=pltpu.SMEM)] + [pl.BlockSpec(memory_space=pltpu.HBM)] * 3,
+        in_specs=[pl.BlockSpec(memory_space=pltpu.HBM)] * 4,
         out_specs=[vmem] * 2,
         out_shape=[jax.ShapeDtypeStruct((OWN, CHUNK, 128), t) for t in (F32, BF)],
         scratch_shapes=[
+            pltpu.SMEM(plan.shape, jnp.int32),
             pltpu.VMEM((2 * TD, 128, 128), BF),
             pltpu.VMEM(blocks.shape, BF),
             pltpu.VMEM((SPARE + 1, 128, 128), F32),
             pltpu.VMEM((7 * 128, 128), F32),
-            pltpu.SemaphoreType.DMA((2 * TD // STEP + 1,)),
+            pltpu.SemaphoreType.DMA((2 * TD // STEP + 2,)),
         ],
         compiler_params=pltpu.CompilerParams(vmem_limit_bytes=40 << 20),
         cost_estimate=pl.CostEstimate(flops=4 * TD * 128**3, bytes_accessed=18 << 20, transcendentals=0),
@@ -187,17 +188,25 @@
     )(place, keep, came)
 
 
-def pair_kernel(keep, came, out):
-    out[...] = (keep[...] + came[...].astype(F32)).astype(BF)
-
-
-def pair_sums(keep, came):
+def pair_kernel(place, keep, came, out):
+    for core in range(2):
+        for parity in range(2):
+
+            @pl.when((place[0] == core) & (place[1] == parity))
+            def _():
+                for k, j in enumerate(ORDER[core][parity]):
+                    out[k] = (keep[j] + came[j].astype(F32)).astype(BF)
+
+
+def pair_sums(place, keep, came):
+    vmem = pl.BlockSpec(memory_space=pltpu.VMEM)
     return pl.pallas_call(
         pair_kernel,
+        in_specs=[pl.BlockSpec(memory_space=pltpu.SMEM), vmem, vmem],
         out_shape=jax.ShapeDtypeStruct(keep.shape, BF),
         compiler_params=pltpu.CompilerParams(vmem_limit_bytes=16 << 20),
         name="pair_sums",
-    )(keep, came)
+    )(place, keep, came)
 
 
 def last_kernel(parts, tiles, feats):
@@ -218,22 +227,24 @@
     )(parts)
 
 
-def own_sums(send, keep):
+def own_sums(place, send, keep):
     trade = []
     for d in range(32):
         for z in range(OWN):
             up = z % 2 == d % 2
             trade.append((d * OWN + z, d * OWN + (z + (1 if up else -1)) % OWN))
-    mid = pair_sums(keep, lax.ppermute(send, ("dom", "own"), trade))
-    groups = [[2 * k + b for k in range(HALF)] for b in range(2)]
-    return last_sums(lax.all_to_all(mid, "own", 0, 0, tiled=True, axis_index_groups=groups))
+    mid = pair_sums(place, keep, lax.ppermute(send, ("dom", "own"), trade))
+    groups = []
+    for d in range(32):
+        groups += [[d * OWN + 2 * k + b for k in ORDER[d % 2][b]] for b in range(2)]
+    return last_sums(lax.all_to_all(mid, ("dom", "own"), 0, 0, tiled=True, axis_index_groups=groups))
 
 
 def gather(copies):
     over_x = [[[8 * y + 2 * x + c for x in range(4)] for y in range(4)] for c in range(2)]
     over_y = [[[8 * y + 2 * x + c for y in range(4)] for x in range(4)] for c in range(2)]
     nearby = lax.all_to_all(copies, "dom", 0, 0, tiled=True, axis_index_groups=over_x[0] + over_y[1])
-    copies = jnp.tile(nearby, (4, 1, 1))
+    copies = four_times(nearby)
     return lax.all_to_all(copies, "dom", 0, 0, tiled=True, axis_index_groups=over_y[0] + over_x[1])
 
 
@@ -243,7 +254,7 @@
 
 
 def local(tiles, prolong, features, match, row_local, col_dom, col_local, coarse_slot, tile_count):
-    copies = four_copies(prolong, features)
+    copies = jnp.tile(jnp.concatenate([prolong, features], axis=2), (4, 1, 1))
     left = left_products(row_local, tile_count, prolong, tiles, copies)
     last = jnp.concatenate([match, tile_count, jnp.zeros((tiles.shape[0] - BD - 1,), jnp.int32)])
     mine = jnp.stack([places(col_dom[:, 0], col_local), coarse_slot, row_local, last])
@@ -254,7 +265,7 @@
     plan = plan_products(place, mine, theirs)
     keep, give = column_products(plan, left, left_theirs, blocks)
     stay, send = fold_sums(place, keep, lax.ppermute(give, "dom", swap))
-    return own_sums(send, stay)
+    return own_sums(place, send, stay)
 
 
 def solution(mesh):

time: 146 us -> 138 us (0.945); the launches traced: 146 us -> 135 us
  blocking collectives: 69.9 us -> 58.9 us
  Pallas kernels: 15.2 us -> 19.8 us
  waiting for transfers between devices: 38.1 us -> 35.6 us
  local copies, waits for them, and re-layouts: 6.57 us -> 4.1 us
    all_to_all x1, blocking collectives: 50 us -> 39 us  [own_sums(): lax.all_to_all(mid, ('dom', 'own'), 0, 0, tiled=True, axis_index_groups=g...]
    another operation x1, local copies, waits for them, and re-layouts: 3.39 us -> 0.16 us  [local(): copies = jnp.tile(jnp.concatenate([prolong, features], axis=2), (4, 1, 1))]
    all_to_all x1, waiting for transfers between devices: 22.3 us -> 19.9 us  [gather(): lax.all_to_all(copies, 'dom', 0, 0, tiled=True, axis_index_groups=over_y[...]
    pallas_call x3, Pallas kernels: 6.61 us -> 8.71 us  [the longest x1 7.53 us: column_products(): pl.pallas_call(column_kernel, in_specs=[pl.BlockSpec(memory_space=pltpu.H...]
    pallas_call x1, Pallas kernels: 2.53 us -> 4.35 us  [plan_products(): pl.pallas_call(plan_kernel, in_specs=[smem] * 3, out_specs=smem, out_shap...]
    unnamed x24 -> x22, local copies, waits for them, and re-layouts: 3.17 us -> 3.94 us
  transfers between devices with their start and end apart: 5 -> 5, of which waited for: 4 -> 4; matrix products, arithmetic and copies ran while one was open for 0% -> 1% of each run, Pallas kernels for 5% -> 7%
where the time goes in v5:
time: 138 us; the launch traced here: 135 us
  blocking collectives  58.9 us (43%)
  waiting for transfers between devices  35.6 us (26%)
  Pallas kernels  19.8 us (14%)
  starting transfers between devices  13.5 us (10%)
  local copies, waits for them, and re-layouts  4.1 us (3%)
  other arithmetic  1.84 us (1%)
  between operations  1.49 us (1%)
    all_to_all x1, blocking collectives, own_sums(): lax.all_to_all(mid, ('dom', 'own'), 0, 0, tiled=True, axis_index_groups=g...  39 us
    all_to_all x1, blocking collectives, gather(): lax.all_to_all(copies, 'dom', 0, 0, tiled=True, axis_index_groups=over_x[...  19.9 us
    all_to_all x1, waiting for transfers between devices, gather(): lax.all_to_all(copies, 'dom', 0, 0, tiled=True, axis_index_groups=over_y[...  19.9 us
    ppermute x1, waiting for transfers between devices, own_sums(): mid = pair_sums(place, keep, lax.ppermute(send, ('dom', 'own'), trade))  9.85 us
    pallas_call x1, Pallas kernels, column_products(): pl.pallas_call(column_kernel, in_specs=[pl.BlockSpec(memory_space=pltpu.H...  7.53 us
    all_to_all x1, starting transfers between devices, gather(): lax.all_to_all(copies, 'dom', 0, 0, tiled=True, axis_index_groups=over_y[...  5.39 us
    pallas_call x1, Pallas kernels, left_products(): pl.pallas_call(left_kernel, grid_spec=pltpu.PrefetchScalarGridSpec(num_sc...  5.21 us
    pallas_call x1, Pallas kernels, plan_products(): pl.pallas_call(plan_kernel, in_specs=[smem] * 3, out_specs=smem, out_shap...  4.35 us
  transfers between devices with their start and end apart: 5, of which 4 were waited for; matrix products, arithmetic and copies ran while one was open for 1% of the time, Pallas kernels for 7%

profile of v5, /device:TPU:6, one launch (start us, length us, event | category | flops | bytes accessed | tf_op | source)
XLA Modules:
  0.0 135.3 jit_solution(11202973452428045898)
XLA Ops:
  0.6 1.1 pad_maximum_fusion
  1.7 0.2 tile.4
  1.9 19.9 %all_to_all.15.nearby = bf16[24,128,256]{2,1,0:T(8,128)(2,1)S(1)} all-to-all(bf16[24,128,256]{2,1,0:T(8,128)(2,1)S(1)} %bitcast.29), channel_id=1, replica_groups={{0,32,64,96},{128,160,192,224},{256,288,320,352},{384,416,448,480},{16,..., dimensions={0} | all-to-all | bytes 3145728 | tf_op jit(solution)/shard_map/all_to_all | solution.py:246
  21.8 0.5 four_times.1
  22.3 2.6 %copy-done = bf16[4,24,128,256]{3,2,1,0:T(8,128)(2,1)} copy-done((bf16[4,24,128,256]{3,2,1,0:T(8,128)(2,1)}, bf16[4,24,128,256]{3,2,1,0:T(8,128)(2,1)S(1)}, u32[]{:S(2)}) %copy-start) | copy-done | bytes 6291480
  25.0 5.4 %all-to-all-start.1 = ((bf16[96,128,256]{2,1,0:T(8,128)(2,1)}), bf16[96,128,256]{2,1,0:T(8,128)(2,1)}, u32[]{:S(2)}, u32[]{:S(2)}) async-start(bf16[96,128,256]{2,1,0:T(8,128)(2,1)} %bitcast.28), calls=%async_computation.1 | async-start | bytes 12582912 | tf_op jit(solution)/shard_map/all_to_all | solution.py:248
  31.1 5.2 %left_products.1.left = bf16[112,128,128]{2,1,0:T(8,128)(2,1)} custom-call(s32[112]{0:T(128)S(1)} %copy-done.4, s32[1]{0:T(128)S(6)} %copy.11.count, bf16[6,128,128]{2,1,0:T(8,128)(2,1)S(1)} %copy-done.1, bf16[112,128,128]{2,1,0:T(8,128)(2,1)} %tiles.1, bf16[24,128,256]{2,1,0:T(8,128)(2,1)S(1)} %bitcast.30), custom_call_target="tpu_custom_call" | custom-call | flops 469762048 | bytes 7340032 | tf_op jit(solution)/shard_map/left_products/pallas_call | solution.py:43
  36.3 1.9 %collective-permute-start.1 = (bf16[112,128,128]{2,1,0:T(8,128)(2,1)}, bf16[112,128,128]{2,1,0:T(8,128)(2,1)}, u32[]{:S(2)}, u32[]{:S(2)}) collective-permute-start(bf16[112,128,128]{2,1,0:T(8,128)(2,1)} %left_products.1.left), channel_id=1, source_target_pairs={{0,16},{16,0},{32,48},{48,32},{64,80},{80,64},{96,112},{112,96},{1... | collective-permute-start | bytes 11010056 | tf_op jit(solution)/shard_map/ppermute | solution.py:262
  38.4 2.4 %collective-permute-start = (s32[4,112]{1,0:T(4,128)S(1)}, s32[4,112]{1,0:T(4,128)S(1)}, u32[]{:S(2)}, u32[]{:S(2)}) collective-permute-start(s32[4,112]{1,0:T(4,128)S(1)} %pad_add_fusion.mine), channel_id=1, source_target_pairs={{0,16},{16,0},{32,48},{48,32},{64,80},{80,64},{96,112},{112,96},{1... | collective-permute-start | bytes 5384 | tf_op jit(solution)/shard_map/ppermute | solution.py:262
  40.8 0.7 pad_add_fusion.1.place
  41.5 3.1 %collective-permute-done.theirs = s32[4,112]{1,0:T(4,128)S(1)} collective-permute-done((s32[4,112]{1,0:T(4,128)S(1)}, s32[4,112]{1,0:T(4,128)S(1)}, u32[]{:S(2)}, u32[]{:S(2)}) %collective-permute-start) | collective-permute-done | bytes 1824 | tf_op jit(solution)/shard_map/ppermute | solution.py:262
  44.6 0.6 copy-done.6
  45.2 4.3 %plan_products.1.planned = s32[4,256]{1,0:T(4,128)} custom-call(s32[2]{0:T(128)} %pad_add_fusion.1.place, s32[4,112]{1,0:T(4,128)} %copy-done.5, s32[4,112]{1,0:T(4,128)} %copy-done.6), custom_call_target="tpu_custom_call" | custom-call | tf_op jit(solution)/shard_map/plan_products/pallas_call | solution.py:106
  49.5 19.9 %all-to-all-done.1.blocks = bf16[96,128,256]{2,1,0:T(8,128)(2,1)} async-done(((bf16[96,128,256]{2,1,0:T(8,128)(2,1)}), bf16[96,128,256]{2,1,0:T(8,128)(2,1)}, u32[]{:S(2)}, u32[]{:S(2)}) %all-to-all-start.1) | async-done | bytes 6291488 | tf_op jit(solution)/shard_map/all_to_all | solution.py:248
  69.4 0.7 copy-done.2
  70.1 7.5 %column_products.1 = (f32[16,288,128]{2,1,0:T(8,128)S(1)}, bf16[16,288,128]{2,1,0:T(8,128)(2,1)S(1)}) custom-call(s32[4,256]{1,0:T(4,128)S(1)} %copy-done.2, bf16[112,128,128]{2,1,0:T(8,128)(2,1)} %left_products.1.left, bf16[112,128,128]{2,1,0:T(8,128)(2,1)} %collective-permute-done.1.left_theirs, bf16[96,128,256]{2,1,0:T(8,128)(2,1)} %all-to-all-done.1.blocks), custom_call_target="tpu_custom_call" | custom-call | flops 939524096 | bytes 18874368 | tf_op jit(solution)/shard_map/column_products/pallas_call | solution.py:152
  77.6 1.9 %collective-permute-start.2 = (bf16[16,288,128]{2,1,0:T(8,128)(2,1)S(1)}, bf16[16,288,128]{2,1,0:T(8,128)(2,1)S(1)}, u32[]{:S(2)}, u32[]{:S(2)}) collective-permute-start(bf16[16,288,128]{2,1,0:T(8,128)(2,1)S(1)} %get-tuple-element.7), channel_id=1, source_target_pairs={{0,16},{16,0},{32,48},{48,32},{64,80},{80,64},{96,112},{112,96},{1... | collective-permute-start | bytes 3538952 | tf_op jit(solution)/shard_map/ppermute | solution.py:267
  79.5 2.8 %collective-permute-done.2.came = bf16[16,288,128]{2,1,0:T(8,128)(2,1)S(1)} collective-permute-done((bf16[16,288,128]{2,1,0:T(8,128)(2,1)S(1)}, bf16[16,288,128]{2,1,0:T(8,128)(2,1)S(1)}, u32[]{:S(2)}, u32[]{:S(2)}) %collective-permute-start.2) | collective-permute-done | bytes 1179680 | tf_op jit(solution)/shard_map/ppermute | solution.py:267
  82.4 0.8 fold_sums.1
  83.1 1.9 %collective-permute-start.3 = (bf16[8,288,128]{2,1,0:T(8,128)(2,1)S(1)}, bf16[8,288,128]{2,1,0:T(8,128)(2,1)S(1)}, u32[]{:S(2)}, u32[]{:S(2)}) collective-permute-start(bf16[8,288,128]{2,1,0:T(8,128)(2,1)S(1)} %get-tuple-element.9), channel_id=1, source_target_pairs={{0,1},{1,0},{2,3},{3,2},{4,5},{5,4},{6,7},{7,6},{8,9},{9,8},{10,11... | collective-permute-start | bytes 1769480 | tf_op jit(solution)/shard_map/ppermute | solution.py:236
  85.1 9.8 %collective-permute-done.3.came = bf16[8,288,128]{2,1,0:T(8,128)(2,1)S(1)} collective-permute-done((bf16[8,288,128]{2,1,0:T(8,128)(2,1)S(1)}, bf16[8,288,128]{2,1,0:T(8,128)(2,1)S(1)}, u32[]{:S(2)}, u32[]{:S(2)}) %collective-permute-start.3) | collective-permute-done | bytes 589856 | tf_op jit(solution)/shard_map/ppermute | solution.py:236
  94.9 0.7 pair_sums.1
  95.6 39.0 %all_to_all.16.parts = bf16[8,288,128]{2,1,0:T(8,128)(2,1)S(1)} all-to-all(bf16[8,288,128]{2,1,0:T(8,128)(2,1)S(1)} %pair_sums.1), channel_id=1, replica_groups={{0,2,4,6,8,10,12,14},{9,11,13,15,1,3,5,7},{24,26,28,30,16,18,20,22},{17..., dimensions={0} | all-to-all | bytes 1179648 | tf_op jit(solution)/shard_map/all_to_all | solution.py:240
  134.6 0.7 last_sums.1
  (24 shorter events, 0.2 us)
Async XLA Ops:
  22.3 2.6 %copy-start = (bf16[4,24,128,256]{3,2,1,0:T(8,128)(2,1)}, bf16[4,24,128,256]{3,2,1,0:T(8,128)(2,1)S(1)}, u32[]{:S(2)}) copy-start(bf16[4,24,128,256]{3,2,1,0:T(8,128)(2,1)S(1)} %four_times.1) | copy-start | bytes 18874372
  24.9 6.0 %copy-start.1 = (bf16[6,128,128]{2,1,0:T(8,128)(2,1)S(1)}, bf16[6,128,128]{2,1,0:T(8,128)(2,1)}, u32[]{:S(2)}) copy-start(bf16[6,128,128]{2,1,0:T(8,128)(2,1)} %prolong.1) | copy-start | bytes 589828
  25.0 6.1 %copy-start.4 = (s32[112]{0:T(128)S(1)}, s32[112]{0:T(128)}, u32[]{:S(2)}) copy-start(s32[112]{0:T(128)} %rows.1) | copy-start | bytes 1348
  25.0 44.4 %all-to-all-start.1 = ((bf16[96,128,256]{2,1,0:T(8,128)(2,1)}), bf16[96,128,256]{2,1,0:T(8,128)(2,1)}, u32[]{:S(2)}, u32[]{:S(2)}) async-start(bf16[96,128,256]{2,1,0:T(8,128)(2,1)} %bitcast.28), calls=%async_computation.1 | async-start | bytes 12582912 | tf_op jit(solution)/shard_map/all_to_all | solution.py:248
  31.0 7.2 %copy-start.7 = (s32[6]{0:T(128)S(1)}, s32[6]{0:T(128)}, u32[]{:S(2)}) copy-start(s32[6]{0:T(128)} %param.12) | copy-start | bytes 76
  31.0 7.3 %copy-start.9 = (s32[112]{0:T(128)S(1)}, s32[112]{0:T(128)}, u32[]{:S(2)}) copy-start(s32[112]{0:T(128)} %param.15) | copy-start | bytes 1348
  31.0 7.3 %copy-start.10 = (s32[112,1]{0,1:T(1,128)S(1)}, s32[112,1]{0,1:T(1,128)}, u32[]{:S(2)}) copy-start(s32[112,1]{0,1:T(1,128)} %param.14) | copy-start | bytes 1348
  31.1 7.3 %copy-start.8 = (s32[112]{0:T(128)S(1)}, s32[112]{0:T(128)}, u32[]{:S(2)}) copy-start(s32[112]{0:T(128)} %param.16) | copy-start | bytes 1348
  36.3 13.2 %collective-permute-start.1 = (bf16[112,128,128]{2,1,0:T(8,128)(2,1)}, bf16[112,128,128]{2,1,0:T(8,128)(2,1)}, u32[]{:S(2)}, u32[]{:S(2)}) collective-permute-start(bf16[112,128,128]{2,1,0:T(8,128)(2,1)} %left_products.1.left), channel_id=1, source_target_pairs={{0,16},{16,0},{32,48},{48,32},{64,80},{80,64},{96,112},{112,96},{1... | collective-permute-start | bytes 11010056 | tf_op jit(solution)/shard_map/ppermute | solution.py:262
  38.3 6.2 %copy-start.5 = (s32[4,112]{1,0:T(4,128)}, s32[4,112]{1,0:T(4,128)S(1)}, u32[]{:S(2)}) copy-start(s32[4,112]{1,0:T(4,128)S(1)} %pad_add_fusion.mine) | copy-start | bytes 5380
  38.4 6.2 %collective-permute-start = (s32[4,112]{1,0:T(4,128)S(1)}, s32[4,112]{1,0:T(4,128)S(1)}, u32[]{:S(2)}, u32[]{:S(2)}) collective-permute-start(s32[4,112]{1,0:T(4,128)S(1)} %pad_add_fusion.mine), channel_id=1, source_target_pairs={{0,16},{16,0},{32,48},{48,32},{64,80},{80,64},{96,112},{112,96},{1... | collective-permute-start | bytes 5384 | tf_op jit(solution)/shard_map/ppermute | solution.py:262
  44.6 0.6 copy-start.6
  45.2 37.2 %copy-start.3 = (s32[2]{0:T(128)S(1)}, s32[2]{0:T(128)}, u32[]{:S(2)}) copy-start(s32[2]{0:T(128)} %pad_add_fusion.1.place) | copy-start | bytes 28
  69.4 0.7 copy-start.2
  77.6 4.7 %collective-permute-start.2 = (bf16[16,288,128]{2,1,0:T(8,128)(2,1)S(1)}, bf16[16,288,128]{2,1,0:T(8,128)(2,1)S(1)}, u32[]{:S(2)}, u32[]{:S(2)}) collective-permute-start(bf16[16,288,128]{2,1,0:T(8,128)(2,1)S(1)} %get-tuple-element.7), channel_id=1, source_target_pairs={{0,16},{16,0},{32,48},{48,32},{64,80},{80,64},{96,112},{112,96},{1... | collective-permute-start | bytes 3538952 | tf_op jit(solution)/shard_map/ppermute | solution.py:267
  83.1 11.8 %collective-permute-start.3 = (bf16[8,288,128]{2,1,0:T(8,128)(2,1)S(1)}, bf16[8,288,128]{2,1,0:T(8,128)(2,1)S(1)}, u32[]{:S(2)}, u32[]{:S(2)}) collective-permute-start(bf16[8,288,128]{2,1,0:T(8,128)(2,1)S(1)} %get-tuple-element.9), channel_id=1, source_target_pairs={{0,1},{1,0},{2,3},{3,2},{4,5},{5,4},{6,7},{7,6},{8,9},{9,8},{10,11... | collective-permute-start | bytes 1769480 | tf_op jit(solution)/shard_map/ppermute | solution.py:236

commit v6 on v5

--- a/solution.py
+++ b/solution.py
@@ -169,11 +169,15 @@
 
 
 def fold_kernel(place, keep, came, stay, send):
-    p = place[1]
-    for k in range(HALF):
-        here, there = 2 * k + p, 2 * k + 1 - p
-        stay[k] = keep[here] + came[here].astype(F32)
-        send[k] = (keep[there] + came[there].astype(F32)).astype(BF)
+    for core in range(2):
+        for p in range(2):
+
+            @pl.when((place[0] == core) & (place[1] == p))
+            def _():
+                for k in range(HALF):
+                    here, there = 2 * ORDER[core][p][k] + p, 2 * ORDER[core][1 - p][k] + 1 - p
+                    stay[k] = keep[here] + came[here].astype(F32)
+                    send[k] = (keep[there] + came[there].astype(F32)).astype(BF)
 
 
 def fold_sums(place, keep, came):
@@ -188,25 +192,17 @@
     )(place, keep, came)
 
 
-def pair_kernel(place, keep, came, out):
-    for core in range(2):
-        for parity in range(2):
-
-            @pl.when((place[0] == core) & (place[1] == parity))
-            def _():
-                for k, j in enumerate(ORDER[core][parity]):
-                    out[k] = (keep[j] + came[j].astype(F32)).astype(BF)
-
-
-def pair_sums(place, keep, came):
-    vmem = pl.BlockSpec(memory_space=pltpu.VMEM)
+def pair_kernel(keep, came, out):
+    out[...] = (keep[...] + came[...].astype(F32)).astype(BF)
+
+
+def pair_sums(keep, came):
     return pl.pallas_call(
         pair_kernel,
-        in_specs=[pl.BlockSpec(memory_space=pltpu.SMEM), vmem, vmem],
         out_shape=jax.ShapeDtypeStruct(keep.shape, BF),
         compiler_params=pltpu.CompilerParams(vmem_limit_bytes=16 << 20),
         name="pair_sums",
-    )(place, keep, came)
+    )(keep, came)
 
 
 def last_kernel(parts, tiles, feats):
@@ -227,13 +223,13 @@
     )(parts)
 
 
-def own_sums(place, send, keep):
+def own_sums(send, keep):
     trade = []
     for d in range(32):
         for z in range(OWN):
             up = z % 2 == d % 2
             trade.append((d * OWN + z, d * OWN + (z + (1 if up else -1)) % OWN))
-    mid = pair_sums(place, keep, lax.ppermute(send, ("dom", "own"), trade))
+    mid = pair_sums(keep, lax.ppermute(send, ("dom", "own"), trade))
     groups = []
     for d in range(32):
         groups += [[d * OWN + 2 * k + b for k in ORDER[d % 2][b]] for b in range(2)]
@@ -265,7 +261,7 @@
     plan = plan_products(place, mine, theirs)
     keep, give = column_products(plan, left, left_theirs, blocks)
     stay, send = fold_sums(place, keep, lax.ppermute(give, "dom", swap))
-    return own_sums(place, send, stay)
+    return own_sums(send, stay)
 
 
 def solution(mesh):

time: 138 us -> 138 us (level)
  Pallas kernels: 19.8 us -> 13.8 us
  blocking collectives: 58.9 us -> 62.2 us
  waiting for transfers between devices: 35.6 us -> 38.8 us
    all_to_all x1, blocking collectives: 39 us -> 42.3 us  [own_sums(): lax.all_to_all(mid, ('dom', 'own'), 0, 0, tiled=True, axis_index_groups=g...]
    all_to_all x1, waiting for transfers between devices: 19.9 us -> 23 us  [gather(): lax.all_to_all(copies, 'dom', 0, 0, tiled=True, axis_index_groups=over_y[...]
    pallas_call x1, Pallas kernels: 7.53 us -> 5.31 us  [column_products(): pl.pallas_call(column_kernel, in_specs=[pl.BlockSpec(memory_space=pltpu.H...]
    pallas_call x1, Pallas kernels: 4.35 us -> 2.76 us  [plan_products(): pl.pallas_call(plan_kernel, in_specs=[smem] * 3, out_specs=smem, out_shap...]
    pallas_call x1, Pallas kernels: 5.21 us -> 3.65 us  [left_products(): pl.pallas_call(left_kernel, grid_spec=pltpu.PrefetchScalarGridSpec(num_sc...]
  transfers between devices with their start and end apart: 5 -> 5, of which waited for: 4 -> 4; matrix products, arithmetic and copies ran while one was open for 1% -> 1% of each run, Pallas kernels for 7% -> 5%
where the time goes in v6:
time: 138 us; the launch traced here: 136 us
  blocking collectives  62.2 us (45%)
  waiting for transfers between devices  38.8 us (28%)
  Pallas kernels  13.8 us (10%)
  starting transfers between devices  13.5 us (10%)
  local copies, waits for them, and re-layouts  4.1 us (3%)
  other arithmetic  1.84 us (1%)
  between operations  1.49 us (1%)
    all_to_all x1, blocking collectives, own_sums(): lax.all_to_all(mid, ('dom', 'own'), 0, 0, tiled=True, axis_index_groups=g...  42.3 us
    all_to_all x1, waiting for transfers between devices, gather(): lax.all_to_all(copies, 'dom', 0, 0, tiled=True, axis_index_groups=over_y[...  23 us
    all_to_all x1, blocking collectives, gather(): lax.all_to_all(copies, 'dom', 0, 0, tiled=True, axis_index_groups=over_x[...  19.9 us
    ppermute x1, waiting for transfers between devices, own_sums(): mid = pair_sums(keep, lax.ppermute(send, ('dom', 'own'), trade))  9.85 us
    all_to_all x1, starting transfers between devices, gather(): lax.all_to_all(copies, 'dom', 0, 0, tiled=True, axis_index_groups=over_y[...  5.39 us
    pallas_call x1, Pallas kernels, column_products(): pl.pallas_call(column_kernel, in_specs=[pl.BlockSpec(memory_space=pltpu.H...  5.31 us
    unnamed x22, local copies, waits for them, and re-layouts  3.94 us
    pallas_call x1, Pallas kernels, left_products(): pl.pallas_call(left_kernel, grid_spec=pltpu.PrefetchScalarGridSpec(num_sc...  3.65 us
  transfers between devices with their start and end apart: 5, of which 4 were waited for; matrix products, arithmetic and copies ran while one was open for 1% of the time, Pallas kernels for 5%

profile of v6, /device:TPU:6, one launch (start us, length us, event | category | flops | bytes accessed | tf_op | source)
XLA Modules:
  0.0 135.8 jit_solution(14746739461976311068)
XLA Ops:
  0.6 1.1 pad_maximum_fusion
  1.7 0.2 tile.4
  1.9 19.9 %all_to_all.15.nearby = bf16[24,128,256]{2,1,0:T(8,128)(2,1)S(1)} all-to-all(bf16[24,128,256]{2,1,0:T(8,128)(2,1)S(1)} %bitcast.29), channel_id=1, replica_groups={{0,32,64,96},{128,160,192,224},{256,288,320,352},{384,416,448,480},{16,..., dimensions={0} | all-to-all | bytes 3145728 | tf_op jit(solution)/shard_map/all_to_all | solution.py:242
  21.8 0.5 four_times.1
  22.3 2.6 %copy-done = bf16[4,24,128,256]{3,2,1,0:T(8,128)(2,1)} copy-done((bf16[4,24,128,256]{3,2,1,0:T(8,128)(2,1)}, bf16[4,24,128,256]{3,2,1,0:T(8,128)(2,1)S(1)}, u32[]{:S(2)}) %copy-start) | copy-done | bytes 6291480
  25.0 5.4 %all-to-all-start.1 = ((bf16[96,128,256]{2,1,0:T(8,128)(2,1)}), bf16[96,128,256]{2,1,0:T(8,128)(2,1)}, u32[]{:S(2)}, u32[]{:S(2)}) async-start(bf16[96,128,256]{2,1,0:T(8,128)(2,1)} %bitcast.28), calls=%async_computation.1 | async-start | bytes 12582912 | tf_op jit(solution)/shard_map/all_to_all | solution.py:244
  31.1 3.6 %left_products.1.left = bf16[112,128,128]{2,1,0:T(8,128)(2,1)} custom-call(s32[112]{0:T(128)S(1)} %copy-done.3, s32[1]{0:T(128)S(6)} %copy.11.count, bf16[6,128,128]{2,1,0:T(8,128)(2,1)S(1)} %copy-done.1, bf16[112,128,128]{2,1,0:T(8,128)(2,1)} %tiles.1, bf16[24,128,256]{2,1,0:T(8,128)(2,1)S(1)} %bitcast.30), custom_call_target="tpu_custom_call" | custom-call | flops 469762048 | bytes 7340032 | tf_op jit(solution)/shard_map/left_products/pallas_call | solution.py:43
  34.7 1.9 %collective-permute-start.1 = (bf16[112,128,128]{2,1,0:T(8,128)(2,1)}, bf16[112,128,128]{2,1,0:T(8,128)(2,1)}, u32[]{:S(2)}, u32[]{:S(2)}) collective-permute-start(bf16[112,128,128]{2,1,0:T(8,128)(2,1)} %left_products.1.left), channel_id=1, source_target_pairs={{0,16},{16,0},{32,48},{48,32},{64,80},{80,64},{96,112},{112,96},{1... | collective-permute-start | bytes 11010056 | tf_op jit(solution)/shard_map/ppermute | solution.py:258
  36.8 2.4 %collective-permute-start = (s32[4,112]{1,0:T(4,128)S(1)}, s32[4,112]{1,0:T(4,128)S(1)}, u32[]{:S(2)}, u32[]{:S(2)}) collective-permute-start(s32[4,112]{1,0:T(4,128)S(1)} %pad_add_fusion.mine), channel_id=1, source_target_pairs={{0,16},{16,0},{32,48},{48,32},{64,80},{80,64},{96,112},{112,96},{1... | collective-permute-start | bytes 5384 | tf_op jit(solution)/shard_map/ppermute | solution.py:258
  39.2 0.7 pad_add_fusion.1.place
  39.9 3.1 %collective-permute-done.theirs = s32[4,112]{1,0:T(4,128)S(1)} collective-permute-done((s32[4,112]{1,0:T(4,128)S(1)}, s32[4,112]{1,0:T(4,128)S(1)}, u32[]{:S(2)}, u32[]{:S(2)}) %collective-permute-start) | collective-permute-done | bytes 1824 | tf_op jit(solution)/shard_map/ppermute | solution.py:258
  43.0 0.6 copy-done.6
  43.6 2.8 %plan_products.1.planned = s32[4,256]{1,0:T(4,128)} custom-call(s32[2]{0:T(128)} %pad_add_fusion.1.place, s32[4,112]{1,0:T(4,128)} %copy-done.5, s32[4,112]{1,0:T(4,128)} %copy-done.6), custom_call_target="tpu_custom_call" | custom-call | tf_op jit(solution)/shard_map/plan_products/pallas_call | solution.py:106
  46.4 23.0 %all-to-all-done.1.blocks = bf16[96,128,256]{2,1,0:T(8,128)(2,1)} async-done(((bf16[96,128,256]{2,1,0:T(8,128)(2,1)}), bf16[96,128,256]{2,1,0:T(8,128)(2,1)}, u32[]{:S(2)}, u32[]{:S(2)}) %all-to-all-start.1) | async-done | bytes 6291488 | tf_op jit(solution)/shard_map/all_to_all | solution.py:244
  69.4 0.7 copy-done.2
  70.1 5.3 %column_products.1 = (f32[16,288,128]{2,1,0:T(8,128)S(1)}, bf16[16,288,128]{2,1,0:T(8,128)(2,1)S(1)}) custom-call(s32[4,256]{1,0:T(4,128)S(1)} %copy-done.2, bf16[112,128,128]{2,1,0:T(8,128)(2,1)} %left_products.1.left, bf16[112,128,128]{2,1,0:T(8,128)(2,1)} %collective-permute-done.1.left_theirs, bf16[96,128,256]{2,1,0:T(8,128)(2,1)} %all-to-all-done.1.blocks), custom_call_target="tpu_custom_call" | custom-call | flops 939524096 | bytes 18874368 | tf_op jit(solution)/shard_map/column_products/pallas_call | solution.py:152
  75.4 1.9 %collective-permute-start.2 = (bf16[16,288,128]{2,1,0:T(8,128)(2,1)S(1)}, bf16[16,288,128]{2,1,0:T(8,128)(2,1)S(1)}, u32[]{:S(2)}, u32[]{:S(2)}) collective-permute-start(bf16[16,288,128]{2,1,0:T(8,128)(2,1)S(1)} %get-tuple-element.7), channel_id=1, source_target_pairs={{0,16},{16,0},{32,48},{48,32},{64,80},{80,64},{96,112},{112,96},{1... | collective-permute-start | bytes 3538952 | tf_op jit(solution)/shard_map/ppermute | solution.py:263
  77.3 2.8 %collective-permute-done.2.came = bf16[16,288,128]{2,1,0:T(8,128)(2,1)S(1)} collective-permute-done((bf16[16,288,128]{2,1,0:T(8,128)(2,1)S(1)}, bf16[16,288,128]{2,1,0:T(8,128)(2,1)S(1)}, u32[]{:S(2)}, u32[]{:S(2)}) %collective-permute-start.2) | collective-permute-done | bytes 1179680 | tf_op jit(solution)/shard_map/ppermute | solution.py:263
  80.1 0.7 fold_sums.1
  80.9 1.9 %collective-permute-start.3 = (bf16[8,288,128]{2,1,0:T(8,128)(2,1)S(1)}, bf16[8,288,128]{2,1,0:T(8,128)(2,1)S(1)}, u32[]{:S(2)}, u32[]{:S(2)}) collective-permute-start(bf16[8,288,128]{2,1,0:T(8,128)(2,1)S(1)} %get-tuple-element.9), channel_id=1, source_target_pairs={{0,1},{1,0},{2,3},{3,2},{4,5},{5,4},{6,7},{7,6},{8,9},{9,8},{10,11... | collective-permute-start | bytes 1769480 | tf_op jit(solution)/shard_map/ppermute | solution.py:232
  82.8 9.8 %collective-permute-done.3.came = bf16[8,288,128]{2,1,0:T(8,128)(2,1)S(1)} collective-permute-done((bf16[8,288,128]{2,1,0:T(8,128)(2,1)S(1)}, bf16[8,288,128]{2,1,0:T(8,128)(2,1)S(1)}, u32[]{:S(2)}, u32[]{:S(2)}) %collective-permute-start.3) | collective-permute-done | bytes 589856 | tf_op jit(solution)/shard_map/ppermute | solution.py:232
  92.7 0.1 pair_sums.1
  92.8 42.3 %all_to_all.16.parts = bf16[8,288,128]{2,1,0:T(8,128)(2,1)S(1)} all-to-all(bf16[8,288,128]{2,1,0:T(8,128)(2,1)S(1)} %pair_sums.1), channel_id=1, replica_groups={{0,2,4,6,8,10,12,14},{9,11,13,15,1,3,5,7},{24,26,28,30,16,18,20,22},{17..., dimensions={0} | all-to-all | bytes 1179648 | tf_op jit(solution)/shard_map/all_to_all | solution.py:236
  135.1 0.7 last_sums.1
  (24 shorter events, 0.2 us)
Async XLA Ops:
  22.3 2.6 %copy-start = (bf16[4,24,128,256]{3,2,1,0:T(8,128)(2,1)}, bf16[4,24,128,256]{3,2,1,0:T(8,128)(2,1)S(1)}, u32[]{:S(2)}) copy-start(bf16[4,24,128,256]{3,2,1,0:T(8,128)(2,1)S(1)} %four_times.1) | copy-start | bytes 18874372
  24.9 6.0 %copy-start.1 = (bf16[6,128,128]{2,1,0:T(8,128)(2,1)S(1)}, bf16[6,128,128]{2,1,0:T(8,128)(2,1)}, u32[]{:S(2)}) copy-start(bf16[6,128,128]{2,1,0:T(8,128)(2,1)} %prolong.1) | copy-start | bytes 589828
  25.0 6.1 %copy-start.3 = (s32[112]{0:T(128)S(1)}, s32[112]{0:T(128)}, u32[]{:S(2)}) copy-start(s32[112]{0:T(128)} %rows.1) | copy-start | bytes 1348
  25.0 44.4 %all-to-all-start.1 = ((bf16[96,128,256]{2,1,0:T(8,128)(2,1)}), bf16[96,128,256]{2,1,0:T(8,128)(2,1)}, u32[]{:S(2)}, u32[]{:S(2)}) async-start(bf16[96,128,256]{2,1,0:T(8,128)(2,1)} %bitcast.28), calls=%async_computation.1 | async-start | bytes 12582912 | tf_op jit(solution)/shard_map/all_to_all | solution.py:244
  31.0 5.6 %copy-start.7 = (s32[6]{0:T(128)S(1)}, s32[6]{0:T(128)}, u32[]{:S(2)}) copy-start(s32[6]{0:T(128)} %param.12) | copy-start | bytes 76
  31.0 5.7 %copy-start.9 = (s32[112]{0:T(128)S(1)}, s32[112]{0:T(128)}, u32[]{:S(2)}) copy-start(s32[112]{0:T(128)} %param.15) | copy-start | bytes 1348
  31.0 5.7 %copy-start.10 = (s32[112,1]{0,1:T(1,128)S(1)}, s32[112,1]{0,1:T(1,128)}, u32[]{:S(2)}) copy-start(s32[112,1]{0,1:T(1,128)} %param.14) | copy-start | bytes 1348
  31.1 5.7 %copy-start.8 = (s32[112]{0:T(128)S(1)}, s32[112]{0:T(128)}, u32[]{:S(2)}) copy-start(s32[112]{0:T(128)} %param.16) | copy-start | bytes 1348
  34.7 11.7 %collective-permute-start.1 = (bf16[112,128,128]{2,1,0:T(8,128)(2,1)}, bf16[112,128,128]{2,1,0:T(8,128)(2,1)}, u32[]{:S(2)}, u32[]{:S(2)}) collective-permute-start(bf16[112,128,128]{2,1,0:T(8,128)(2,1)} %left_products.1.left), channel_id=1, source_target_pairs={{0,16},{16,0},{32,48},{48,32},{64,80},{80,64},{96,112},{112,96},{1... | collective-permute-start | bytes 11010056 | tf_op jit(solution)/shard_map/ppermute | solution.py:258
  36.8 6.2 %copy-start.5 = (s32[4,112]{1,0:T(4,128)}, s32[4,112]{1,0:T(4,128)S(1)}, u32[]{:S(2)}) copy-start(s32[4,112]{1,0:T(4,128)S(1)} %pad_add_fusion.mine) | copy-start | bytes 5380
  36.8 6.2 %collective-permute-start = (s32[4,112]{1,0:T(4,128)S(1)}, s32[4,112]{1,0:T(4,128)S(1)}, u32[]{:S(2)}, u32[]{:S(2)}) collective-permute-start(s32[4,112]{1,0:T(4,128)S(1)} %pad_add_fusion.mine), channel_id=1, source_target_pairs={{0,16},{16,0},{32,48},{48,32},{64,80},{80,64},{96,112},{112,96},{1... | collective-permute-start | bytes 5384 | tf_op jit(solution)/shard_map/ppermute | solution.py:258
  43.0 0.6 copy-start.6
  43.6 36.5 %copy-start.4 = (s32[2]{0:T(128)S(1)}, s32[2]{0:T(128)}, u32[]{:S(2)}) copy-start(s32[2]{0:T(128)} %pad_add_fusion.1.place) | copy-start | bytes 28
  69.4 0.7 copy-start.2
  75.4 4.7 %collective-permute-start.2 = (bf16[16,288,128]{2,1,0:T(8,128)(2,1)S(1)}, bf16[16,288,128]{2,1,0:T(8,128)(2,1)S(1)}, u32[]{:S(2)}, u32[]{:S(2)}) collective-permute-start(bf16[16,288,128]{2,1,0:T(8,128)(2,1)S(1)} %get-tuple-element.7), channel_id=1, source_target_pairs={{0,16},{16,0},{32,48},{48,32},{64,80},{80,64},{96,112},{112,96},{1... | collective-permute-start | bytes 3538952 | tf_op jit(solution)/shard_map/ppermute | solution.py:263
  80.9 11.8 %collective-permute-start.3 = (bf16[8,288,128]{2,1,0:T(8,128)(2,1)S(1)}, bf16[8,288,128]{2,1,0:T(8,128)(2,1)S(1)}, u32[]{:S(2)}, u32[]{:S(2)}) collective-permute-start(bf16[8,288,128]{2,1,0:T(8,128)(2,1)S(1)} %get-tuple-element.9), channel_id=1, source_target_pairs={{0,1},{1,0},{2,3},{3,2},{4,5},{5,4},{6,7},{7,6},{8,9},{9,8},{10,11... | collective-permute-start | bytes 1769480 | tf_op jit(solution)/shard_map/ppermute | solution.py:232

commit v7 on v6

--- a/solution.py
+++ b/solution.py
@@ -14,6 +14,7 @@
 CHUNK = 288
 STEP = 16
 UNROLL = 16
+REST = 4
 BF = jnp.bfloat16
 ORDER = [[[0, 1, 2, 3, 4, 5, 6, 7], [4, 5, 6, 7, 0, 1, 2, 3]], [[4, 5, 6, 7, 0, 1, 2, 3], [0, 1, 2, 3, 4, 5, 6, 7]]]
 F32 = jnp.float32
@@ -131,14 +132,24 @@
         pl.when(live)(move.wait)
     whole.wait()
 
-    @pl.loop(0, pl.cdiv(plan[0, PLAN - 1], UNROLL))
-    def _(i):
-        for u in range(UNROLL):
-            n = i * UNROLL + u
+    def add(first, number):
+        for u in range(number):
+            n = first + u
             both = jnp.dot(held_l[plan[0, n]], held_b[plan[1, n]], preferred_element_type=F32)
             rows = pl.ds(pl.multiple_of(plan[3, n], 128), 128)
             sums[plan[2, n]] += both[:, :128]
             feats[rows, :] += both[:, 128:]
+
+    chosen = plan[0, PLAN - 1]
+    full = chosen // UNROLL
+
+    @pl.loop(0, full)
+    def _(i):
+        add(i * UNROLL, UNROLL)
+
+    @pl.loop(0, pl.cdiv(chosen - full * UNROLL, REST))
+    def _(i):
+        add(full * UNROLL + i * REST, REST)
 
     for d, ref in enumerate((keep, give)):
         for o in range(OWN):

time: 138 us -> 137 us (level)
  no operation moved by 1% of the time
where the time goes in v7:
time: 137 us; the launch traced here: 136 us
  blocking collectives  62.5 us (46%)
  waiting for transfers between devices  38 us (28%)
  Pallas kernels  14.6 us (11%)
  starting transfers between devices  13.5 us (10%)
  local copies, waits for them, and re-layouts  4.1 us (3%)
  other arithmetic  1.84 us (1%)
  between operations  1.49 us (1%)
    all_to_all x1, blocking collectives, own_sums(): lax.all_to_all(mid, ('dom', 'own'), 0, 0, tiled=True, axis_index_groups=g...  42.6 us
    all_to_all x1, waiting for transfers between devices, gather(): lax.all_to_all(copies, 'dom', 0, 0, tiled=True, axis_index_groups=over_y[...  22.2 us
    all_to_all x1, blocking collectives, gather(): lax.all_to_all(copies, 'dom', 0, 0, tiled=True, axis_index_groups=over_x[...  19.9 us
    ppermute x1, waiting for transfers between devices, own_sums(): mid = pair_sums(keep, lax.ppermute(send, ('dom', 'own'), trade))  9.85 us
    all_to_all x1, starting transfers between devices, gather(): lax.all_to_all(copies, 'dom', 0, 0, tiled=True, axis_index_groups=over_y[...  5.39 us
    pallas_call x1, Pallas kernels, column_products(): pl.pallas_call(column_kernel, in_specs=[pl.BlockSpec(memory_space=pltpu.H...  5.37 us
    pallas_call x1, Pallas kernels, left_products(): pl.pallas_call(left_kernel, grid_spec=pltpu.PrefetchScalarGridSpec(num_sc...  4.62 us
    unnamed x22, local copies, waits for them, and re-layouts  3.94 us
  transfers between devices with their start and end apart: 5, of which 4 were waited for; matrix products, arithmetic and copies ran while one was open for 1% of the time, Pallas kernels for 5%

profile of v7, /device:TPU:6, one launch (start us, length us, event | category | flops | bytes accessed | tf_op | source)
XLA Modules:
  0.0 136.2 jit_solution(12405441096541634284)
XLA Ops:
  0.6 1.1 pad_maximum_fusion
  1.7 0.2 tile.4
  1.9 19.9 %all_to_all.15.nearby = bf16[24,128,256]{2,1,0:T(8,128)(2,1)S(1)} all-to-all(bf16[24,128,256]{2,1,0:T(8,128)(2,1)S(1)} %bitcast.29), channel_id=1, replica_groups={{0,32,64,96},{128,160,192,224},{256,288,320,352},{384,416,448,480},{16,..., dimensions={0} | all-to-all | bytes 3145728 | tf_op jit(solution)/shard_map/all_to_all | solution.py:253
  21.8 0.5 four_times.1
  22.3 2.6 %copy-done = bf16[4,24,128,256]{3,2,1,0:T(8,128)(2,1)} copy-done((bf16[4,24,128,256]{3,2,1,0:T(8,128)(2,1)}, bf16[4,24,128,256]{3,2,1,0:T(8,128)(2,1)S(1)}, u32[]{:S(2)}) %copy-start) | copy-done | bytes 6291480
  25.0 5.4 %all-to-all-start.1 = ((bf16[96,128,256]{2,1,0:T(8,128)(2,1)}), bf16[96,128,256]{2,1,0:T(8,128)(2,1)}, u32[]{:S(2)}, u32[]{:S(2)}) async-start(bf16[96,128,256]{2,1,0:T(8,128)(2,1)} %bitcast.28), calls=%async_computation.1 | async-start | bytes 12582912 | tf_op jit(solution)/shard_map/all_to_all | solution.py:255
  31.1 4.6 %left_products.1.left = bf16[112,128,128]{2,1,0:T(8,128)(2,1)} custom-call(s32[112]{0:T(128)S(1)} %copy-done.3, s32[1]{0:T(128)S(6)} %copy.11.count, bf16[6,128,128]{2,1,0:T(8,128)(2,1)S(1)} %copy-done.1, bf16[112,128,128]{2,1,0:T(8,128)(2,1)} %tiles.1, bf16[24,128,256]{2,1,0:T(8,128)(2,1)S(1)} %bitcast.30), custom_call_target="tpu_custom_call" | custom-call | flops 469762048 | bytes 7340032 | tf_op jit(solution)/shard_map/left_products/pallas_call | solution.py:44
  35.7 1.9 %collective-permute-start.1 = (bf16[112,128,128]{2,1,0:T(8,128)(2,1)}, bf16[112,128,128]{2,1,0:T(8,128)(2,1)}, u32[]{:S(2)}, u32[]{:S(2)}) collective-permute-start(bf16[112,128,128]{2,1,0:T(8,128)(2,1)} %left_products.1.left), channel_id=1, source_target_pairs={{0,16},{16,0},{32,48},{48,32},{64,80},{80,64},{96,112},{112,96},{1... | collective-permute-start | bytes 11010056 | tf_op jit(solution)/shard_map/ppermute | solution.py:269
  37.8 2.4 %collective-permute-start = (s32[4,112]{1,0:T(4,128)S(1)}, s32[4,112]{1,0:T(4,128)S(1)}, u32[]{:S(2)}, u32[]{:S(2)}) collective-permute-start(s32[4,112]{1,0:T(4,128)S(1)} %pad_add_fusion.mine), channel_id=1, source_target_pairs={{0,16},{16,0},{32,48},{48,32},{64,80},{80,64},{96,112},{112,96},{1... | collective-permute-start | bytes 5384 | tf_op jit(solution)/shard_map/ppermute | solution.py:269
  40.2 0.7 pad_add_fusion.1.place
  40.9 3.1 %collective-permute-done.theirs = s32[4,112]{1,0:T(4,128)S(1)} collective-permute-done((s32[4,112]{1,0:T(4,128)S(1)}, s32[4,112]{1,0:T(4,128)S(1)}, u32[]{:S(2)}, u32[]{:S(2)}) %collective-permute-start) | collective-permute-done | bytes 1824 | tf_op jit(solution)/shard_map/ppermute | solution.py:269
  44.0 0.6 copy-done.6
  44.6 2.6 %plan_products.1.planned = s32[4,256]{1,0:T(4,128)} custom-call(s32[2]{0:T(128)} %pad_add_fusion.1.place, s32[4,112]{1,0:T(4,128)} %copy-done.5, s32[4,112]{1,0:T(4,128)} %copy-done.6), custom_call_target="tpu_custom_call" | custom-call | tf_op jit(solution)/shard_map/plan_products/pallas_call | solution.py:107
  47.2 22.2 %all-to-all-done.1.blocks = bf16[96,128,256]{2,1,0:T(8,128)(2,1)} async-done(((bf16[96,128,256]{2,1,0:T(8,128)(2,1)}), bf16[96,128,256]{2,1,0:T(8,128)(2,1)}, u32[]{:S(2)}, u32[]{:S(2)}) %all-to-all-start.1) | async-done | bytes 6291488 | tf_op jit(solution)/shard_map/all_to_all | solution.py:255
  69.4 0.7 copy-done.2
  70.1 5.4 %column_products.1 = (f32[16,288,128]{2,1,0:T(8,128)S(1)}, bf16[16,288,128]{2,1,0:T(8,128)(2,1)S(1)}) custom-call(s32[4,256]{1,0:T(4,128)S(1)} %copy-done.2, bf16[112,128,128]{2,1,0:T(8,128)(2,1)} %left_products.1.left, bf16[112,128,128]{2,1,0:T(8,128)(2,1)} %collective-permute-done.1.left_theirs, bf16[96,128,256]{2,1,0:T(8,128)(2,1)} %all-to-all-done.1.blocks), custom_call_target="tpu_custom_call" | custom-call | flops 939524096 | bytes 18874368 | tf_op jit(solution)/shard_map/column_products/pallas_call | solution.py:163
  75.4 1.9 %collective-permute-start.2 = (bf16[16,288,128]{2,1,0:T(8,128)(2,1)S(1)}, bf16[16,288,128]{2,1,0:T(8,128)(2,1)S(1)}, u32[]{:S(2)}, u32[]{:S(2)}) collective-permute-start(bf16[16,288,128]{2,1,0:T(8,128)(2,1)S(1)} %get-tuple-element.7), channel_id=1, source_target_pairs={{0,16},{16,0},{32,48},{48,32},{64,80},{80,64},{96,112},{112,96},{1... | collective-permute-start | bytes 3538952 | tf_op jit(solution)/shard_map/ppermute | solution.py:274
  77.4 2.8 %collective-permute-done.2.came = bf16[16,288,128]{2,1,0:T(8,128)(2,1)S(1)} collective-permute-done((bf16[16,288,128]{2,1,0:T(8,128)(2,1)S(1)}, bf16[16,288,128]{2,1,0:T(8,128)(2,1)S(1)}, u32[]{:S(2)}, u32[]{:S(2)}) %collective-permute-start.2) | collective-permute-done | bytes 1179680 | tf_op jit(solution)/shard_map/ppermute | solution.py:274
  80.2 0.7 fold_sums.1
  81.0 1.9 %collective-permute-start.3 = (bf16[8,288,128]{2,1,0:T(8,128)(2,1)S(1)}, bf16[8,288,128]{2,1,0:T(8,128)(2,1)S(1)}, u32[]{:S(2)}, u32[]{:S(2)}) collective-permute-start(bf16[8,288,128]{2,1,0:T(8,128)(2,1)S(1)} %get-tuple-element.9), channel_id=1, source_target_pairs={{0,1},{1,0},{2,3},{3,2},{4,5},{5,4},{6,7},{7,6},{8,9},{9,8},{10,11... | collective-permute-start | bytes 1769480 | tf_op jit(solution)/shard_map/ppermute | solution.py:243
  82.9 9.8 %collective-permute-done.3.came = bf16[8,288,128]{2,1,0:T(8,128)(2,1)S(1)} collective-permute-done((bf16[8,288,128]{2,1,0:T(8,128)(2,1)S(1)}, bf16[8,288,128]{2,1,0:T(8,128)(2,1)S(1)}, u32[]{:S(2)}, u32[]{:S(2)}) %collective-permute-start.3) | collective-permute-done | bytes 589856 | tf_op jit(solution)/shard_map/ppermute | solution.py:243
  92.7 0.1 pair_sums.1
  92.8 42.6 %all_to_all.16.parts = bf16[8,288,128]{2,1,0:T(8,128)(2,1)S(1)} all-to-all(bf16[8,288,128]{2,1,0:T(8,128)(2,1)S(1)} %pair_sums.1), channel_id=1, replica_groups={{0,2,4,6,8,10,12,14},{9,11,13,15,1,3,5,7},{24,26,28,30,16,18,20,22},{17..., dimensions={0} | all-to-all | bytes 1179648 | tf_op jit(solution)/shard_map/all_to_all | solution.py:247
  135.4 0.7 last_sums.1
  (24 shorter events, 0.2 us)
Async XLA Ops:
  22.3 2.6 %copy-start = (bf16[4,24,128,256]{3,2,1,0:T(8,128)(2,1)}, bf16[4,24,128,256]{3,2,1,0:T(8,128)(2,1)S(1)}, u32[]{:S(2)}) copy-start(bf16[4,24,128,256]{3,2,1,0:T(8,128)(2,1)S(1)} %four_times.1) | copy-start | bytes 18874372
  24.9 6.0 %copy-start.1 = (bf16[6,128,128]{2,1,0:T(8,128)(2,1)S(1)}, bf16[6,128,128]{2,1,0:T(8,128)(2,1)}, u32[]{:S(2)}) copy-start(bf16[6,128,128]{2,1,0:T(8,128)(2,1)} %prolong.1) | copy-start | bytes 589828
  25.0 6.1 %copy-start.3 = (s32[112]{0:T(128)S(1)}, s32[112]{0:T(128)}, u32[]{:S(2)}) copy-start(s32[112]{0:T(128)} %rows.1) | copy-start | bytes 1348
  25.0 44.4 %all-to-all-start.1 = ((bf16[96,128,256]{2,1,0:T(8,128)(2,1)}), bf16[96,128,256]{2,1,0:T(8,128)(2,1)}, u32[]{:S(2)}, u32[]{:S(2)}) async-start(bf16[96,128,256]{2,1,0:T(8,128)(2,1)} %bitcast.28), calls=%async_computation.1 | async-start | bytes 12582912 | tf_op jit(solution)/shard_map/all_to_all | solution.py:255
  31.0 6.6 %copy-start.7 = (s32[6]{0:T(128)S(1)}, s32[6]{0:T(128)}, u32[]{:S(2)}) copy-start(s32[6]{0:T(128)} %param.12) | copy-start | bytes 76
  31.0 6.7 %copy-start.9 = (s32[112]{0:T(128)S(1)}, s32[112]{0:T(128)}, u32[]{:S(2)}) copy-start(s32[112]{0:T(128)} %param.15) | copy-start | bytes 1348
  31.0 6.7 %copy-start.10 = (s32[112,1]{0,1:T(1,128)S(1)}, s32[112,1]{0,1:T(1,128)}, u32[]{:S(2)}) copy-start(s32[112,1]{0,1:T(1,128)} %param.14) | copy-start | bytes 1348
  31.1 6.7 %copy-start.8 = (s32[112]{0:T(128)S(1)}, s32[112]{0:T(128)}, u32[]{:S(2)}) copy-start(s32[112]{0:T(128)} %param.16) | copy-start | bytes 1348
  35.7 11.5 %collective-permute-start.1 = (bf16[112,128,128]{2,1,0:T(8,128)(2,1)}, bf16[112,128,128]{2,1,0:T(8,128)(2,1)}, u32[]{:S(2)}, u32[]{:S(2)}) collective-permute-start(bf16[112,128,128]{2,1,0:T(8,128)(2,1)} %left_products.1.left), channel_id=1, source_target_pairs={{0,16},{16,0},{32,48},{48,32},{64,80},{80,64},{96,112},{112,96},{1... | collective-permute-start | bytes 11010056 | tf_op jit(solution)/shard_map/ppermute | solution.py:269
  37.8 6.2 %copy-start.5 = (s32[4,112]{1,0:T(4,128)}, s32[4,112]{1,0:T(4,128)S(1)}, u32[]{:S(2)}) copy-start(s32[4,112]{1,0:T(4,128)S(1)} %pad_add_fusion.mine) | copy-start | bytes 5380
  37.8 6.2 %collective-permute-start = (s32[4,112]{1,0:T(4,128)S(1)}, s32[4,112]{1,0:T(4,128)S(1)}, u32[]{:S(2)}, u32[]{:S(2)}) collective-permute-start(s32[4,112]{1,0:T(4,128)S(1)} %pad_add_fusion.mine), channel_id=1, source_target_pairs={{0,16},{16,0},{32,48},{48,32},{64,80},{80,64},{96,112},{112,96},{1... | collective-permute-start | bytes 5384 | tf_op jit(solution)/shard_map/ppermute | solution.py:269
  44.0 0.6 copy-start.6
  44.6 35.6 %copy-start.4 = (s32[2]{0:T(128)S(1)}, s32[2]{0:T(128)}, u32[]{:S(2)}) copy-start(s32[2]{0:T(128)} %pad_add_fusion.1.place) | copy-start | bytes 28
  69.4 0.7 copy-start.2
  75.4 4.7 %collective-permute-start.2 = (bf16[16,288,128]{2,1,0:T(8,128)(2,1)S(1)}, bf16[16,288,128]{2,1,0:T(8,128)(2,1)S(1)}, u32[]{:S(2)}, u32[]{:S(2)}) collective-permute-start(bf16[16,288,128]{2,1,0:T(8,128)(2,1)S(1)} %get-tuple-element.7), channel_id=1, source_target_pairs={{0,16},{16,0},{32,48},{48,32},{64,80},{80,64},{96,112},{112,96},{1... | collective-permute-start | bytes 3538952 | tf_op jit(solution)/shard_map/ppermute | solution.py:274
  81.0 11.8 %collective-permute-start.3 = (bf16[8,288,128]{2,1,0:T(8,128)(2,1)S(1)}, bf16[8,288,128]{2,1,0:T(8,128)(2,1)S(1)}, u32[]{:S(2)}, u32[]{:S(2)}) collective-permute-start(bf16[8,288,128]{2,1,0:T(8,128)(2,1)S(1)} %get-tuple-element.9), channel_id=1, source_target_pairs={{0,1},{1,0},{2,3},{3,2},{4,5},{5,4},{6,7},{7,6},{8,9},{9,8},{10,11... | collective-permute-start | bytes 1769480 | tf_op jit(solution)/shard_map/ppermute | solution.py:243
